TPU v7x, 512 devices: a whole 4x4x16 slice. The times are simulated.
512 devices in a mesh: gx: 16 (over z), gy: 8 (over y, core), gz: 4 (over x).
Axes of the slice: x: 4, y: 4, z: 16, core: 2. Of those that a mesh axis runs over, the one named last changes fastest.
Arguments:
- coords: float32 [3, 524288], P(None, ('gx', 'gy', 'gz')), may hold values from 0 to 256, as said below
- polarizability: float32 [524288], P(('gx', 'gy', 'gz')), may hold values from 0.05 to 0.2
- external_field: float32 [3, 524288], P(None, ('gx', 'gy', 'gz')), may hold values from -1000 to 1000
- bead_live: int32 [524288], P(('gx', 'gy', 'gz')), may hold values from 0 to 1, as said below
- ghost_x: int32 [2, 131072], P(None, ('gx', 'gy', 'gz')), may hold values from 0 to 1023, as said below
- ghost_y: int32 [2, 393216], P(None, ('gx', 'gy', 'gz')), may hold values from 0 to 1535, as said below
- ghost_z: int32 [2, 1572864], P(None, ('gx', 'gy', 'gz')), may hold values from 0 to 3071, as said below
- pair_blocks: int32 [2, 110592], P(None, ('gx', 'gy', 'gz')), may hold values from 0 to 71, as said below
- pair_live: int32 [110592], P(('gx', 'gy', 'gz')), may hold values from 0 to 1, as said below
Outputs:
- dipoles: float32 [3, 524288], P(None, ('gx', 'gy', 'gz'))
- dipole_residual: float32 [3, 524288], P(None, ('gx', 'gy', 'gz'))
Inputs may be any that keep to these rules, and one draw needn't show every extreme that they name: `coords`: beads sit near the sites of a cubic lattice of spacing 1: a brick is 16 x 4 * 2 x 8 sites at (16 i, 4 * 2 j, 8 * k), block b = 4-site column group (b // 2, b % 2) of 4 x 4 x 8 sites; every two beads, images included, are 0.6 or more apart. `bead_live`: the owned beads of a device are its first slots; some device owns all 1024 in every draw. `ghost_x`: each row lists every entry of the brick's face layer once, in any order. `ghost_y`: each row lists every entry of a face layer of the set after the gx section once, in any order. `ghost_z`: each row lists every entry of a layer of the set after the gy section once, in any order. `pair_blocks`: A device lists, for each of its blocks that holds an owned bead, the 27 blocks of the extended set beside it or equal to it, in any order, before all padding slots (zeros); some device fills all 216 slots in every draw. `pair_live`: ones first.
All inputs are finite; a program needn't handle non-finite values.
Results may differ from a plain program's by a relative error of at most 0.008.
Values sent between devices are 32-bit elements; how exact they have to be, the bound alone decides.
A program may use at most 64 MiB of HBM per device.

v0:
```python
import jax
import jax.numpy as jnp
from jax import lax
from jax.sharding import PartitionSpec as P

BZ = 8
BY = 2
ITERS = 3
BLOCK = 128


CUTOFF_SQUARED = 12.25
THOLE_FACTOR = 0.02


def passed_along(value, axis, steps):
    count = lax.axis_size(axis)
    pairs = [(source, (source + steps) % count) for source in range(count)]
    return lax.ppermute(value, axis, pairs)


def pair_field(target_geo, source_geo, source_mu, same_block):
    width = target_geo.shape[-1]
    delta_x = target_geo[0][:, :, None] - source_geo[0][:, None, :]
    delta_y = target_geo[1][:, :, None] - source_geo[1][:, None, :]
    delta_z = target_geo[2][:, :, None] - source_geo[2][:, None, :]
    diagonal_lane = jnp.arange(width)[:, None] == jnp.arange(width)[None, :]
    self_pair = jnp.logical_and(same_block, diagonal_lane[None])
    dist_sq = jnp.where(self_pair, 1.0, delta_x * delta_x + delta_y * delta_y + delta_z * delta_z)
    inverse = lax.rsqrt(dist_sq)
    inverse_cube = inverse * inverse * inverse
    margin = jnp.maximum(1.0 - dist_sq / CUTOFF_SQUARED, 0.0)
    taper = jnp.where(self_pair, 0.0, margin * margin)
    scaled = (
        THOLE_FACTOR
        * dist_sq
        * jnp.sqrt(dist_sq)
        * lax.rsqrt(target_geo[3][:, :, None] * source_geo[3][:, None, :])
    )
    damping = jnp.exp(-scaled)
    inner = taper * (1.0 - damping) * inverse_cube
    outer = 3.0 * taper * (1.0 - (1.0 + scaled) * damping) * inverse_cube * inverse * inverse
    moment_x = source_mu[0][:, None, :]
    moment_y = source_mu[1][:, None, :]
    moment_z = source_mu[2][:, None, :]
    along = delta_x * moment_x + delta_y * moment_y + delta_z * moment_z
    field_x = jnp.sum(outer * along * delta_x - inner * moment_x, axis=2)
    field_y = jnp.sum(outer * along * delta_y - inner * moment_y, axis=2)
    field_z = jnp.sum(outer * along * delta_z - inner * moment_z, axis=2)
    return jnp.stack([field_x, field_y, field_z])


def spread(values, ghost_x, ghost_y, ghost_z, boxed):
    ghosted = values
    pieces = [ghosted]
    extent = 16.0 * lax.axis_size("gx")
    for slot_index, offset in enumerate((1, -1)):
        arrived = passed_along(jnp.take(ghosted, ghost_x[slot_index], axis=1), "gx", offset)
        if boxed:
            border = 0 if offset == 1 else lax.axis_size("gx") - 1
            arrived = arrived.at[0].add(
                jnp.where(lax.axis_index("gx") == border, -offset * extent, 0.0)
            )
        pieces.append(arrived)
    ghosted = jnp.concatenate(pieces, axis=1)
    pieces = [ghosted]
    extent = 4.0 * BY * lax.axis_size("gy")
    for slot_index, offset in enumerate((1, -1)):
        arrived = passed_along(jnp.take(ghosted, ghost_y[slot_index], axis=1), "gy", offset)
        if boxed:
            border = 0 if offset == 1 else lax.axis_size("gy") - 1
            arrived = arrived.at[1].add(
                jnp.where(lax.axis_index("gy") == border, -offset * extent, 0.0)
            )
        pieces.append(arrived)
    ghosted = jnp.concatenate(pieces, axis=1)
    pieces = [ghosted]
    extent = 1.0 * BZ * lax.axis_size("gz")
    for slot_index, offset in enumerate((1, -1)):
        arrived = passed_along(jnp.take(ghosted, ghost_z[slot_index], axis=1), "gz", offset)
        if boxed:
            border = 0 if offset == 1 else lax.axis_size("gz") - 1
            arrived = arrived.at[2].add(
                jnp.where(lax.axis_index("gz") == border, -offset * extent, 0.0)
            )
        pieces.append(arrived)
    return jnp.concatenate(pieces, axis=1)


def field_pass(geo_pool, moments, targets, sources, weights, first, last):
    count = weights.shape[0] // 27
    geo_blocks = geo_pool.reshape(4, -1, BLOCK)
    moment_blocks = moments.reshape(3, -1, BLOCK)
    columns = jnp.arange(count)

    def accumulate(group_index, fields):
        start = group_index * count
        target_ids = lax.dynamic_slice_in_dim(targets, start, count)
        source_ids = lax.dynamic_slice_in_dim(sources, start, count)
        weight_row = lax.dynamic_slice_in_dim(weights, start, count)
        contrib = pair_field(
            jnp.take(geo_blocks, target_ids, axis=1),
            jnp.take(geo_blocks, source_ids, axis=1),
            jnp.take(moment_blocks, source_ids, axis=1),
            (target_ids == source_ids)[:, None, None],
        )
        contrib = contrib * weight_row[None, :, None]
        one_hot = (target_ids[:, None] == columns[None, :]).astype(jnp.float32)
        return fields + jnp.einsum("cgb,gn->cnb", contrib, one_hot, precision=lax.Precision.HIGHEST)

    start_fields = jnp.zeros((3, count, BLOCK), jnp.float32)
    return lax.fori_loop(first, last, accumulate, start_fields).reshape(3, -1)


def global_sum(value):
    return lax.psum(value, ("gx", "gy", "gz"))


def per_device(
    coords,
    polarizability,
    external_field,
    bead_live,
    ghost_x,
    ghost_y,
    ghost_z,
    pair_blocks,
    pair_live,
):
    nblk = coords.shape[1] // BLOCK
    living = bead_live.astype(jnp.float32)
    geometry = jnp.concatenate([coords, polarizability[None]], axis=0)
    geo_pool = spread(geometry, ghost_x, ghost_y, ghost_z, True)
    targets = pair_blocks[0]
    sources = pair_blocks[1]
    weights = pair_live.astype(jnp.float32)
    groups = (jnp.sum(pair_live) + nblk - 1) // nblk
    rhs = living * external_field
    dipoles = jnp.zeros_like(rhs)
    residual = rhs
    direction = rhs
    norm_now = global_sum(jnp.sum(residual * residual))
    for iteration in range(ITERS):
        moments = spread(direction, ghost_x, ghost_y, ghost_z, False)
        fields = field_pass(geo_pool, moments, targets, sources, weights, 0, groups)
        image = living * (direction / polarizability[None] - fields)
        step_size = norm_now / lax.psum(jnp.sum(direction * image), ("gx", "gy", "gz"))
        dipoles = dipoles + step_size * direction
        residual = residual - step_size * image
        norm_next = global_sum(jnp.sum(residual * residual))
        direction = residual + norm_next / norm_now * direction
        norm_now = norm_next
    return (dipoles, polarizability[None] * residual)


def solution(mesh):
    placed = (
        P(None, ("gx", "gy", "gz")),
        P(("gx", "gy", "gz")),
        P(None, ("gx", "gy", "gz")),
        P(("gx", "gy", "gz")),
        P(None, ("gx", "gy", "gz")),
        P(None, ("gx", "gy", "gz")),
        P(None, ("gx", "gy", "gz")),
        P(None, ("gx", "gy", "gz")),
        P(("gx", "gy", "gz")),
    )
    return jax.shard_map(
        per_device,
        mesh=mesh,
        in_specs=placed,
        out_specs=(P(None, ("gx", "gy", "gz")), P(None, ("gx", "gy", "gz"))),
        check_vma=False,
    )
```

profile of v0, /device:TPU:1, one launch (start us, length us, event | category | flops | bytes accessed | tf_op | source)
XLA Modules:
  0.0 1125.4 jit_solution(12339648157052791543)
XLA Ops:
  4.5 4.4 collective-permute-start
  10.4 9.5 collective-permute-start.1
  25.7 4.6 collective-permute-start.7
  66.4 10.9 gather_fusion.19
  84.0 11.9 %gather_fusion.20 = f32[3072,3]{1,0:T(8,128)} fusion(f32[3,3072]{0,1:T(8,128)S(1)} %copy.186, s32[3072]{0:T(1024)} %get-tuple-element.573), kind=kCustom, calls=%fused_computation.21.clone | custom fusion | bytes 86016 | tf_op jit(solution)/shard_map/jit(_take)/gather | solution.py:80
  113.9 10.9 gather_fusion.13
  124.8 9.5 gather_fusion.14
  141.4 4.6 collective-permute-start.5
  148.3 70.5 %while.39 = (s32[]{:T(128)}, f32[3,8,128]{2,1,0:T(8,128)S(1)}, s32[]{:T(128)}, s32[216]{0:T(256)S(1)}, s32[216]{0:T(256)S(1)}, /*index=5*/f32[4,72,128]{2,0,1:T(...) while((s32[]{:T(128)}, f32[3,8,128]{2,1,0:T(8,128)S(1)}, ...), condition=%wide.region_7.16_spmd.clone, body=%wide.region_3.15_spmd.clone.sunk | while | flops 7018694 | bytes 406251 | solution.py:112
  219.5 144.8 %all-reduce = (f32[]{:T(128)}, f32[]{:T(128)}) all-reduce(f32[]{:T(128)} %get-tuple-element.424, f32[]{:T(128)} %get-tuple-element.423), channel_id=1, replica_groups=mesh['gx'=16,'gy'=8,'gz'=4] {'gx','gy','gz'}, use_global_device_ids=true, to_apply=%region_1.2 | all-reduce | flops 2 | bytes 16 | tf_op jit(solution)/shard_map/psum | solution.py:116
  366.2 100.4 %psum.44 = f32[]{:T(128)} all-reduce(f32[]{:T(128)} %multiply_reduce_fusion.3), channel_id=1, replica_groups=mesh['gx'=16,'gy'=8,'gz'=4] {'gx','gy','gz'}, use_global_device_ids=true, to_apply=%region_11.20 | all-reduce | flops 1 | bytes 8 | tf_op jit(solution)/shard_map/psum | solution.py:116
  472.0 4.6 collective-permute-start.13
  487.8 10.9 gather_fusion.25
  498.7 8.1 gather_fusion.26
  514.0 4.6 collective-permute-start.17
  519.8 81.8 %while.40 = (s32[]{:T(128)}, f32[3,8,128]{2,1,0:T(8,128)S(1)}, s32[]{:T(128)}, s32[216]{0:T(256)S(1)}, s32[216]{0:T(256)S(1)}, /*index=5*/f32[4,72,128]{2,0,1:T(...) while((s32[]{:T(128)}, f32[3,8,128]{2,1,0:T(8,128)S(1)}, ...), condition=%wide.region_16.25_spmd.clone, body=%wide.region_12.24_spmd.clone.sunk | while | flops 7018694 | bytes 406251 | solution.py:112
  602.3 151.0 %psum.45 = f32[]{:T(128)} all-reduce(f32[]{:T(128)} %multiply_reduce_fusion.2), channel_id=1, replica_groups=mesh['gx'=16,'gy'=8,'gz'=4] {'gx','gy','gz'}, use_global_device_ids=true, to_apply=%region_18.27 | all-reduce | flops 1 | bytes 8 | tf_op jit(solution)/shard_map/psum | solution.py:147
  755.2 99.3 %psum.46 = f32[]{:T(128)} all-reduce(f32[]{:T(128)} %get-tuple-element.491), channel_id=1, replica_groups=mesh['gx'=16,'gy'=8,'gz'=4] {'gx','gy','gz'}, use_global_device_ids=true, to_apply=%region_20.29 | all-reduce | flops 1 | bytes 8 | tf_op jit(solution)/shard_map/psum | solution.py:116
  857.9 3.5 collective-permute-start.18
  876.6 10.9 gather_fusion.31
  887.5 8.1 gather_fusion.32
  902.9 4.6 collective-permute-start.23
  908.7 70.2 %while.41 = (s32[]{:T(128)}, f32[3,8,128]{2,1,0:T(8,128)S(1)}, s32[]{:T(128)}, s32[216]{0:T(256)S(1)}, s32[216]{0:T(256)S(1)}, /*index=5*/f32[4,72,128]{2,0,1:T(...) while((s32[]{:T(128)}, f32[3,8,128]{2,1,0:T(8,128)S(1)}, ...), condition=%wide.region_25.34_spmd.clone, body=%wide.region_21.33_spmd.clone.sunk | while | flops 7018694 | bytes 406251 | solution.py:112
  979.5 144.0 %psum.47 = f32[]{:T(128)} all-reduce(f32[]{:T(128)} %multiply_reduce_fusion), channel_id=1, replica_groups=mesh['gx'=16,'gy'=8,'gz'=4] {'gx','gy','gz'}, use_global_device_ids=true, to_apply=%region_27.36 | all-reduce | flops 1 | bytes 8 | tf_op jit(solution)/shard_map/psum | solution.py:147
  (1218 shorter events, 351.5 us)
Async XLA Ops:
  4.5 46.6 %collective-permute-start = (f32[4,256]{0,1:T(8,128)}, f32[4,256]{0,1:T(8,128)S(1)}, u32[]{:S(2)}, u32[]{:S(2)}) collective-permute-start(f32[4,256]{0,1:T(8,128)} %select_bitcast_fusion.20), channel_id=1, source_target_pairs={{0,32},{32,64},{64,96},{96,128},{128,160},{160,192},{192,224},{224... | collective-permute-start | bytes 12296 | tf_op jit(solution)/shard_map/ppermute | solution.py:19
  10.4 41.9 %collective-permute-start.1 = (f32[4,256]{0,1:T(8,128)}, f32[4,256]{0,1:T(8,128)S(1)}, u32[]{:S(2)}, u32[]{:S(2)}) collective-permute-start(f32[4,256]{0,1:T(8,128)} %select_bitcast_fusion.19), channel_id=1, source_target_pairs={{0,480},{32,0},{64,32},{96,64},{128,96},{160,128},{192,160},{224,1... | collective-permute-start | bytes 12296 | tf_op jit(solution)/shard_map/ppermute | solution.py:19
  23.0 14.1 %collective-permute-start.6 = (f32[3,256]{1,0:T(4,128)S(1)}, f32[3,256]{1,0:T(4,128)S(1)}, u32[]{:S(2)}, u32[]{:S(2)}) collective-permute-start(f32[3,256]{1,0:T(4,128)S(1)} %select_bitcast_fusion.32), channel_id=1, source_target_pairs={{0,32},{32,64},{64,96},{96,128},{128,160},{160,192},{192,224},{224... | collective-permute-start | bytes 9224 | tf_op jit(solution)/shard_map/ppermute | solution.py:19
  25.7 11.4 %collective-permute-start.7 = (f32[3,256]{1,0:T(4,128)S(1)}, f32[3,256]{1,0:T(4,128)S(1)}, u32[]{:S(2)}, u32[]{:S(2)}) collective-permute-start(f32[3,256]{1,0:T(4,128)S(1)} %select_bitcast_fusion.31), channel_id=1, source_target_pairs={{0,480},{32,0},{64,32},{96,64},{128,96},{160,128},{192,160},{224,1... | collective-permute-start | bytes 9224 | tf_op jit(solution)/shard_map/ppermute | solution.py:19
  42.5 20.7 %collective-permute-start.8 = (f32[3,768]{1,0:T(4,128)}, f32[3,768]{1,0:T(4,128)}, u32[]{:S(2)}, u32[]{:S(2)}) collective-permute-start(f32[3,768]{1,0:T(4,128)} %select_bitcast_fusion.26), channel_id=1, source_target_pairs={{0,4},{4,8},{8,12},{12,16},{16,20},{20,24},{24,28},{28,0},{1,5},{5... | collective-permute-start | bytes 27656 | tf_op jit(solution)/shard_map/ppermute | solution.py:19
  48.5 16.0 %collective-permute-start.9 = (f32[3,768]{1,0:T(4,128)}, f32[3,768]{1,0:T(4,128)}, u32[]{:S(2)}, u32[]{:S(2)}) collective-permute-start(f32[3,768]{1,0:T(4,128)} %select_bitcast_fusion.25), channel_id=1, source_target_pairs={{0,28},{4,0},{8,4},{12,8},{16,12},{20,16},{24,20},{28,24},{1,29},{... | collective-permute-start | bytes 27656 | tf_op jit(solution)/shard_map/ppermute | solution.py:19
  58.6 44.3 %collective-permute-start.2 = (f32[4,768]{0,1:T(8,128)}, f32[4,768]{0,1:T(8,128)}, u32[]{:S(2)}, u32[]{:S(2)}) collective-permute-start(f32[4,768]{0,1:T(8,128)} %select_bitcast_fusion.18), channel_id=1, source_target_pairs={{0,4},{4,8},{8,12},{12,16},{16,20},{20,24},{24,28},{28,0},{1,5},{5... | collective-permute-start | bytes 36872 | tf_op jit(solution)/shard_map/ppermute | solution.py:19
  62.0 46.2 %collective-permute-start.3 = (f32[4,768]{0,1:T(8,128)}, f32[4,768]{0,1:T(8,128)S(1)}, u32[]{:S(2)}, u32[]{:S(2)}) collective-permute-start(f32[4,768]{0,1:T(8,128)} %select_bitcast_fusion.17), channel_id=1, source_target_pairs={{0,28},{4,0},{8,4},{12,8},{16,12},{20,16},{24,20},{28,24},{1,29},{... | collective-permute-start | bytes 36872 | tf_op jit(solution)/shard_map/ppermute | solution.py:19
  80.9 65.2 %collective-permute-start.10 = (f32[3,3072]{1,0:T(4,128)}, f32[3,3072]{1,0:T(4,128)}, u32[]{:S(2)}, u32[]{:S(2)}) collective-permute-start(f32[3,3072]{1,0:T(4,128)} %copy.187), channel_id=1, source_target_pairs={{0,1},{1,2},{2,3},{3,0},{4,5},{5,6},{6,7},{7,4},{8,9},{9,10},{10,1... | collective-permute-start | bytes 110600 | tf_op jit(solution)/shard_map/ppermute | solution.py:19
  99.6 47.3 %collective-permute-start.11 = (f32[3,3072]{1,0:T(4,128)}, f32[3,3072]{1,0:T(4,128)}, u32[]{:S(2)}, u32[]{:S(2)}) collective-permute-start(f32[3,3072]{1,0:T(4,128)} %copy.189), channel_id=1, source_target_pairs={{0,3},{1,0},{2,1},{3,2},{4,7},{5,4},{6,5},{7,6},{8,11},{9,8},{10,9... | collective-permute-start | bytes 110600 | tf_op jit(solution)/shard_map/ppermute | solution.py:19
  137.4 10.4 collective-permute-start.4
  141.4 6.6 collective-permute-start.5
  470.0 7.2 collective-permute-start.12
  472.0 5.3 collective-permute-start.13
  481.0 3.5 collective-permute-start.14
  483.3 3.4 collective-permute-start.15
  510.0 8.6 collective-permute-start.16
  514.0 5.7 collective-permute-start.17
  857.9 7.4 collective-permute-start.18
  861.5 4.4 collective-permute-start.19
  869.5 4.1 collective-permute-start.20
  872.4 3.1 collective-permute-start.21
  898.8 8.6 collective-permute-start.22
  902.9 5.7 collective-permute-start.23
  (53 other events, 4015.9 us)
where the time goes:
time: 1130 us
  blocking collectives  640 us (57%)
  local copies, waits for them, and re-layouts  248 us (22%)
  other arithmetic  142 us (13%)
  starting transfers between devices  68.8 us (6%)
    psum x3, blocking collectives, global_sum(): return lax.psum(value, ('gx', 'gy', 'gz'))  345 us
    psum x2, blocking collectives, per_device(): lax.psum(jnp.sum(direction * image), ('gx', 'gy', 'gz'))  295 us
    reduce_sum x51, other arithmetic, pair_field(): field_x = jnp.sum(outer * along * delta_x - inner * moment_x, axis=2)  85.6 us
    gather x8, local copies, waits for them, and re-layouts, spread(): jnp.take(ghosted, ghost_z[slot_index], axis=1)  81.2 us
    ppermute x24, starting transfers between devices, passed_along(): return lax.ppermute(value, axis, pairs)  68.8 us
    gather x51, local copies, waits for them, and re-layouts, accumulate(): jnp.take(moment_blocks, source_ids, axis=1)  29.3 us
    gather x51, local copies, waits for them, and re-layouts, accumulate(): jnp.take(geo_blocks, target_ids, axis=1)  29.3 us
    gather x51, local copies, waits for them, and re-layouts, accumulate(): jnp.take(geo_blocks, source_ids, axis=1)  29.3 us
  transfers between devices with their start and end apart: 24, of which 6 were waited for; matrix products, arithmetic and copies ran while one was open for 10% of the time, Pallas kernels for 0%

commit v1 on v0

v1 whole, which is shorter than its diff:
```python
import functools
import math

import jax
import jax.numpy as jnp
from jax import lax
from jax.experimental import pallas as pl
from jax.experimental.pallas import tpu as pltpu
from jax.sharding import PartitionSpec as P

BLOCK = 128
NBX, NBY = 4, 2
NBLK = NBX * NBY
CX, CY = NBX + 2, NBY + 2
NCOL = CX * CY
GROUP = 32
NGRP = BLOCK // GROUP
BRICK = (16.0, 8.0, 8.0)
CUTOFF_SQUARED = 12.25
THOLE_FACTOR = 0.02
CENTRE, HALF = 12.5, 8.5
FAR = 1.0e6
MESH = pl.DeviceIdType.MESH
HIGHEST = lax.Precision.HIGHEST
OFFSETS = [
    (x, y, z)
    for x in (-1, 0, 1)
    for y in (-1, 0, 1)
    for z in (-1, 0, 1)
    if (x, y, z) != (0, 0, 0)
]
GRAM = [(a, b) for a in range(4) for b in range(a, 4)]


def dot_rows(left, right, precision=HIGHEST):
    return lax.dot_general(
        left, right, (((1,), (0,)), ((), ())), precision=precision,
        preferred_element_type=jnp.float32,
    )


def dot_lanes(left, right, precision=HIGHEST):
    return lax.dot_general(
        left, right, (((1,), (1,)), ((), ())), precision=precision,
        preferred_element_type=jnp.float32,
    )


def iota(shape, axis):
    return lax.broadcasted_iota(jnp.int32, shape, axis)


def own_span(step, count):
    return (0, count) if step == 0 else ((count - 1, 1) if step > 0 else (0, 1))


def halo_span(step, count):
    return (1, count) if step == 0 else ((0, 1) if step > 0 else (count + 1, 1))


def inverse_list(list_ref, row, first, entries, tables):
    blocks = jnp.zeros((tables, BLOCK), jnp.float32)
    lanes = jnp.zeros((tables, BLOCK), jnp.float32)
    spot = iota((BLOCK, BLOCK), 1).astype(jnp.float32)
    for r in range(entries // BLOCK):
        entry = list_ref[row : row + 1, r * BLOCK : (r + 1) * BLOCK]
        high = jnp.right_shift(entry, 7) - first
        low = jnp.bitwise_and(entry, BLOCK - 1)
        pick = (iota((tables, BLOCK), 0) == high).astype(jnp.float32)
        place = (iota((BLOCK, BLOCK), 0) == low).astype(jnp.float32)
        both = jnp.concatenate([place, place * spot], axis=0).astype(jnp.bfloat16)
        found = dot_lanes(pick.astype(jnp.bfloat16), both, None)
        blocks = blocks + found[:, :BLOCK] * float(r + 1)
        lanes = lanes + found[:, BLOCK:]
    return blocks, lanes


def inverse_blocks(list_ref, row, entries):
    rows = entries // BLOCK
    total = jnp.zeros((rows, BLOCK), jnp.float32)
    for r in range(rows):
        entry = list_ref[row : row + 1, r * BLOCK : (r + 1) * BLOCK]
        high = jnp.right_shift(entry, 7)
        low = jnp.bitwise_and(entry, BLOCK - 1)
        pick = jnp.where(iota((rows, BLOCK), 0) == high, float(r), 0.0)
        place = (iota((BLOCK, BLOCK), 0) == low).astype(jnp.float32)
        total = total + dot_lanes(
            pick.astype(jnp.bfloat16), place.astype(jnp.bfloat16), None
        )
    return total


def look_up(table, index):
    high = jnp.right_shift(index, 7)
    low = jnp.bitwise_and(index, BLOCK - 1)
    out = jnp.zeros(index.shape, jnp.float32)
    for r in range(table.shape[0]):
        row = jnp.broadcast_to(table[r : r + 1, :], index.shape)
        out = jnp.where(high == r, jnp.take_along_axis(row, low, axis=1), out)
    return out


def place_of(sizes):
    return tuple(lax.axis_index(name) for name in ("gx", "gy", "gz"))


def neighbour(me, sizes, step):
    return tuple(lax.rem(m + s + n, n) for m, s, n in zip(me, step, sizes))


def greet(targets):
    barrier = pltpu.get_barrier_semaphore()
    for target in targets:
        pl.semaphore_signal(barrier, inc=1, device_id=target, device_id_type=MESH)
    return barrier


def halo_copies(buffer, send_sem, recv_sem, me, sizes):
    copies = []
    for n, step in enumerate(OFFSETS):
        (xs, xn), (ys, yn) = own_span(step[0], NBX), own_span(step[1], NBY)
        (xd, _), (yd, _) = halo_span(step[0], NBX), halo_span(step[1], NBY)
        copies.append(
            pltpu.make_async_remote_copy(
                src_ref=buffer.at[1, pl.ds(1 + xs, xn), pl.ds(1 + ys, yn)],
                dst_ref=buffer.at[1 - step[2], pl.ds(xd, xn), pl.ds(yd, yn)],
                send_sem=send_sem.at[n],
                recv_sem=recv_sem.at[n],
                device_id=neighbour(me, sizes, step),
                device_id_type=MESH,
            )
        )
    return copies


def field_kernel(
    sizes,
    coords, polar, external, live, ghost_x, ghost_y, ghost_z, pairs, alive,
    basis_out, gram_out,
    halo1, halo2, halo3, tabs_y, tabs_z, own_y, own_z, sends, recvs, tab_sends, tab_recvs,
    order, side, target, window, moved, marks, px, py, pz, inner_s, sums, basis,
):
    me = place_of(sizes)
    barrier = greet([neighbour(me, sizes, step) for step in OFFSETS])

    up_blocks, up_lanes = inverse_list(ghost_x, 0, 0, 2 * BLOCK, NBLK)
    down_blocks, down_lanes = inverse_list(ghost_x, 1, 0, 2 * BLOCK, NBLK)
    upper = iota((NBLK, BLOCK), 0) >= NBLK - NBY
    x_spot = jnp.where(
        upper, (up_blocks - 1.0) * BLOCK + up_lanes, (down_blocks - 1.0) * BLOCK + down_lanes
    )
    x_spot = jnp.maximum(x_spot, 0.0)
    lane = iota((1, BLOCK), 1)
    lane_f = lane.astype(jnp.float32)

    for b in range(NBLK):
        cut = slice(b * BLOCK, (b + 1) * BLOCK)
        alpha = polar[0:1, cut]
        living = live[0:1, cut].astype(jnp.float32)
        place = coords[:, cut]
        rhs = external[:, cut] * living
        code = lane_f + x_spot[b : b + 1, :] * BLOCK
        beta = lax.rsqrt(alpha) * math.sqrt(THOLE_FACTOR)
        tile = jnp.concatenate([place, beta, rhs, code], axis=0)
        more = jnp.concatenate(
            [living / alpha, living, jnp.zeros((6, BLOCK), jnp.float32)], axis=0
        )
        column = jnp.transpose(tile)
        z_row = place[2:3, :]
        z_col = column[:, 2:3]
        before = jnp.logical_or(
            z_row < z_col,
            jnp.logical_and(z_row == z_col, iota((BLOCK, BLOCK), 1) < iota((BLOCK, BLOCK), 0)),
        )
        rank = jnp.sum(before.astype(jnp.float32), axis=1, keepdims=True)
        one_hot = (rank == iota((BLOCK, BLOCK), 1).astype(jnp.float32)).astype(jnp.float32)
        order[b] = one_hot
        ranked = dot_rows(jnp.concatenate([tile, more], axis=0), one_hot)
        halo1[1, 1 + b // NBY, 1 + b % NBY] = ranked[:8]
        side[b] = ranked[8:]
        basis[0, b] = jnp.concatenate(
            [ranked[4:7], jnp.zeros((5, BLOCK), jnp.float32)], axis=0
        )
        flipped = jnp.transpose(ranked[:8])
        for g in range(NGRP):
            target[b * NGRP + g] = flipped[g * GROUP : (g + 1) * GROUP]

    pl.semaphore_wait(barrier, len(OFFSETS))
    first = halo_copies(halo1, sends.at[0], recvs.at[0], me, sizes)
    for copy in first:
        copy.start()

    for row in range(2):
        blocks, lanes = inverse_list(ghost_y, row, 0, 6 * BLOCK, 12)
        own_y[row, 0:12] = (blocks - 1.0) * BLOCK + lanes
        own_z[row] = inverse_blocks(ghost_z, row, 24 * BLOCK)
    tables = []
    for row, step_y in enumerate((1, -1)):
        for step_z in (-1, 0, 1):
            n = len(tables)
            tables.append(
                pltpu.make_async_remote_copy(
                    src_ref=own_y.at[row],
                    dst_ref=tabs_y.at[row, 1 - step_z],
                    send_sem=tab_sends.at[n],
                    recv_sem=tab_recvs.at[n],
                    device_id=neighbour(me, sizes, (0, step_y, step_z)),
                    device_id_type=MESH,
                )
            )
    for row, step_z in enumerate((1, -1)):
        n = len(tables)
        tables.append(
            pltpu.make_async_remote_copy(
                src_ref=own_z.at[row],
                dst_ref=tabs_z.at[row],
                send_sem=tab_sends.at[n],
                recv_sem=tab_recvs.at[n],
                device_id=neighbour(me, sizes, (0, 0, step_z)),
                device_id_type=MESH,
            )
        )
    for copy in tables:
        copy.start()

    count = pairs.shape[1]
    bits = jnp.left_shift(alive[0:1, :], pairs[0:1, :]).astype(jnp.float32)
    bits = jnp.broadcast_to(bits, (8, count)).astype(jnp.bfloat16)
    listed = (iota((BLOCK, count), 0) == pairs[1:2, :]).astype(jnp.float32)
    listed_by = dot_lanes(bits, listed.astype(jnp.bfloat16), None)

    for copy in first:
        copy.wait_recv()
    for copy in tables:
        copy.wait_recv()

    for role in range(3):
        for part in range(NCOL // 8):
            codes = jnp.concatenate(
                [
                    halo1[role, c // CY, c % CY, 7:8, :]
                    for c in range(part * 8, part * 8 + 8)
                ],
                axis=0,
            ).astype(jnp.int32)
            spot = jnp.right_shift(codes, 7)
            own_lane = jnp.bitwise_and(codes, BLOCK - 1)
            col = iota((8, BLOCK), 0) + part * 8
            cx, cy = jnp.right_shift(col, 2), jnp.bitwise_and(col, 3)
            block_y = jnp.bitwise_and(cy + 1, 1)
            entry = ((cx - 1) * NBY + block_y) * BLOCK + own_lane
            entry = jnp.where(cx == 0, NBLK * BLOCK + spot, entry)
            entry = jnp.where(cx == CX - 1, (NBLK + NBY) * BLOCK + spot, entry)
            low = look_up(tabs_y[0, role, 0:12], entry)
            high = look_up(tabs_y[1, role, 0:12], entry)
            found = jnp.where(cy == 0, low, jnp.where(cy == CY - 1, high, 0.0))
            valid = found >= 0.0
            found = jnp.maximum(found, 0.0).astype(jnp.int32)
            entry = jnp.where(cy == 0, 12 * BLOCK + found, entry)
            entry = jnp.where(cy == CY - 1, 18 * BLOCK + found, entry)
            if role == 1:
                block = jnp.right_shift(entry, 7)
            else:
                layer = look_up(tabs_z[role // 2], entry)
                block = layer.astype(jnp.int32) + (24 if role == 0 else 48)
            mark = jnp.take_along_axis(listed_by, block, axis=1)
            marks[role, part * 8 : part * 8 + 8] = jnp.where(valid, mark, 0.0)

    row8 = iota((8, BLOCK), 0)
    lane8 = iota((8, BLOCK), 1)
    edge = [
        (jnp.where(m == 0, -n * size, 0.0), jnp.where(m == n - 1, n * size, 0.0))
        for m, n, size in zip(me, sizes, BRICK)
    ]

    def shifted(role, cx, cy):
        tile = halo1[role, cx, cy]
        col = cx * CY + cy
        if cx in (0, CX - 1):
            tile = tile + jnp.where(row8 == 0, edge[0][0 if cx == 0 else 1], 0.0)
        if cy in (0, CY - 1):
            tile = tile + jnp.where(row8 == 1, edge[1][0 if cy == 0 else 1], 0.0)
        if role != 1:
            tile = tile + jnp.where(row8 == 2, edge[2][role // 2], 0.0)
        return jnp.where(row8 == 7, marks[role, col : col + 1, :], tile)

    def windows(below, middle, above, lanes):
        return (
            jnp.where(lanes >= 80, below, middle),
            jnp.where(lanes >= 112, below, middle),
            jnp.where(lanes < 16, above, middle),
            jnp.where(lanes < 48, above, middle),
        )

    for cx in range(CX):
        for cy in range(CY):
            tiles = windows(*[shifted(role, cx, cy) for role in range(3)], lane8)
            for g in range(NGRP):
                window[(cx * CY + cy) * NGRP + g] = tiles[g]

    def build(step, carry):
        block, g = step // NGRP, step % NGRP
        column = (block // NBY) * CY + block % NBY
        mine = target[step]
        tx, ty, tz, tb = [jnp.broadcast_to(mine[:, k : k + 1], (GROUP, BLOCK)) for k in range(4)]
        total = [jnp.zeros((GROUP, BLOCK), jnp.float32) for _ in range(3)]
        for c in range(9):
            tile = window[(column + (c // 3) * CY + c % 3) * NGRP + g]
            bit = jnp.right_shift(tile[7:8].astype(jnp.int32), block)
            seen = jnp.bitwise_and(bit, 1) == 1
            sx = jnp.where(seen, tile[0:1], FAR)
            dx, dy, dz = tx - sx, ty - tile[1:2], tz - tile[2:3]
            if c == 4:
                itself = iota((GROUP, BLOCK), 0) + g * GROUP == iota((GROUP, BLOCK), 1)
                dx = jnp.where(itself, FAR, dx)
            q = dx * dx + dy * dy + dz * dz
            inv = lax.rsqrt(q)
            inv2 = inv * inv
            margin = jnp.maximum(1.0 - q * (1.0 / CUTOFF_SQUARED), 0.0)
            scaled = q * (q * inv) * (tb * tile[3:4])
            damp = jnp.exp(-scaled)
            rest = 1.0 - damp
            inner = (margin * margin) * (inv2 * inv) * rest
            root = (3.0 * inv) * jnp.maximum(rest - scaled * damp, 1e-20)
            scale = margin * inv2 * root * lax.rsqrt(root)
            ax, ay, az = scale * dx, scale * dy, scale * dz
            slot = step * 9 + c
            px[slot], py[slot], pz[slot], inner_s[slot] = ax, ay, az, inner
            vx, vy, vz = tile[4:5], tile[5:6], tile[6:7]
            along = ax * vx + ay * vy + az * vz
            total[0] = total[0] + (along * ax - inner * vx)
            total[1] = total[1] + (along * ay - inner * vy)
            total[2] = total[2] + (along * az - inner * vz)
        for k in range(3):
            sums[block, k, pl.ds(pl.multiple_of(g * GROUP, GROUP), GROUP)] = total[k]
        return carry

    lax.fori_loop(0, NBLK * NGRP, build, 0)

    def apply(step, carry):
        block, g = step // NGRP, step % NGRP
        column = (block // NBY) * CY + block % NBY
        total = [jnp.zeros((GROUP, BLOCK), jnp.float32) for _ in range(3)]
        for c in range(9):
            tile = moved[(column + (c // 3) * CY + c % 3) * NGRP + g]
            slot = step * 9 + c
            ax, ay, az, inner = px[slot], py[slot], pz[slot], inner_s[slot]
            vx, vy, vz = tile[0:1], tile[1:2], tile[2:3]
            along = ax * vx + ay * vy + az * vz
            total[0] = total[0] + (along * ax - inner * vx)
            total[1] = total[1] + (along * ay - inner * vy)
            total[2] = total[2] + (along * az - inner * vz)
        for k in range(3):
            sums[block, k, pl.ds(pl.multiple_of(g * GROUP, GROUP), GROUP)] = total[k]
        return carry

    ones = jnp.ones((8, BLOCK), jnp.float32)

    def next_basis(level, halo):
        for b in range(NBLK):
            field = [dot_lanes(ones, sums[b, k]) for k in range(3)]
            field = jnp.where(row8 == 0, field[0], jnp.where(row8 == 1, field[1], field[2]))
            v = basis[level, b]
            rows = side[b]
            image = rows[0:1] * v - rows[1:2] * field
            image = (image - CENTRE * v) * (1.0 / HALF)
            if level > 0:
                image = 2.0 * image - basis[level - 1, b]
            image = jnp.where(row8 < 3, image, 0.0)
            basis[level + 1, b] = image
            if halo is not None:
                halo[1, 1 + b // NBY, 1 + b % NBY] = image[:4]

    lane4 = iota((4, BLOCK), 1)
    started = first + tables
    for level, halo in ((0, halo2), (1, halo3)):
        next_basis(level, halo)
        copies = halo_copies(halo, sends.at[level + 1], recvs.at[level + 1], me, sizes)
        for copy in copies:
            copy.start()
        for copy in copies:
            copy.wait_recv()
        for cx in range(CX):
            for cy in range(CY):
                tiles = windows(*[halo[role, cx, cy] for role in range(3)], lane4)
                for g in range(NGRP):
                    moved[(cx * CY + cy) * NGRP + g] = tiles[g]
        lax.fori_loop(0, NBLK * NGRP, apply, 0)
        started = started + copies
    next_basis(2, None)

    rows = []
    for a, b in GRAM:
        part = jnp.sum(basis[a] * basis[b], axis=0)
        rows.append(jnp.sum(part, axis=0, keepdims=True))
    rows.append(jnp.zeros((16 - len(GRAM), BLOCK), jnp.float32))
    gram_out[...] = jnp.concatenate(rows, axis=0)
    for b in range(NBLK):
        stacked = jnp.concatenate([basis[k, b] for k in range(4)], axis=0)
        basis_out[:, b * BLOCK : (b + 1) * BLOCK] = dot_lanes(stacked, order[b])
    for copy in started:
        copy.wait_send()


def reduce_kernel(sizes, basis, gram, polar, dipoles, residual, *scratch):
    slots, send_sems, recv_sems = scratch[0:3], scratch[3:6], scratch[6:9]
    me = place_of(sizes)
    partners = []
    for axis, n in enumerate(sizes):
        for s in range(1, n):
            step = [0, 0, 0]
            step[axis] = s
            partners.append(neighbour(me, sizes, step))
    barrier = greet(partners)
    total = gram[...]
    for axis, n in enumerate(sizes):
        slot, send, recv = slots[axis], send_sems[axis], recv_sems[axis]
        slot[me[axis]] = total
        if axis == 0:
            pl.semaphore_wait(barrier, len(partners))
        copies = []
        for s in range(1, n):
            step = [0, 0, 0]
            step[axis] = s
            copies.append(
                pltpu.make_async_remote_copy(
                    src_ref=slot.at[me[axis]],
                    dst_ref=slot.at[me[axis]],
                    send_sem=send.at[s - 1],
                    recv_sem=recv.at[s - 1],
                    device_id=neighbour(me, sizes, step),
                    device_id_type=MESH,
                )
            )
        for copy in copies:
            copy.start()
        for copy in copies:
            copy.wait()
        total = slot[0]
        for k in range(1, n):
            total = total + slot[k]

    whole = jnp.sum(total, axis=1, keepdims=True)
    products = {}
    for k, (a, b) in enumerate(GRAM):
        products[a, b] = products[b, a] = whole[k : k + 1, :]

    def inner(left, right):
        value = 0.0
        for a, p in enumerate(left):
            for b, q in enumerate(right):
                if p is not None and q is not None:
                    value = value + p * q * products[a, b]
        return value

    def plus(p, q):
        return q if p is None else (p if q is None else p + q)

    def times(scale, p):
        return None if p is None else scale * p

    def applied(c):
        out = [times(CENTRE, p) for p in c]
        if c[0] is not None:
            out[1] = plus(out[1], HALF * c[0])
        for k in (1, 2):
            if c[k] is not None:
                out[k - 1] = plus(out[k - 1], (0.5 * HALF) * c[k])
                out[k + 1] = plus(out[k + 1], (0.5 * HALF) * c[k])
        return out

    one = jnp.ones((1, 1), jnp.float32)
    left = [one, None, None, None]
    direction = list(left)
    answer = [None] * 4
    norm = products[0, 0]
    for _ in range(3):
        image = applied(direction)
        step = norm / inner(direction, image)
        answer = [plus(p, times(step, q)) for p, q in zip(answer, direction)]
        left = [plus(p, times(-step, q)) for p, q in zip(left, image)]
        after = inner(left, left)
        direction = [plus(p, times(after / norm, q)) for p, q in zip(left, direction)]
        norm = after

    def combined(coefficients):
        value = 0.0
        for k, c in enumerate(coefficients):
            if c is not None:
                value = value + c * basis[8 * k : 8 * k + 3, :]
        return value

    dipoles[...] = combined(answer)
    residual[...] = polar[...] * combined(left)


def per_device(
    sizes, coords, polarizability, external_field, bead_live,
    ghost_x, ghost_y, ghost_z, pair_blocks, pair_live,
):
    nloc = coords.shape[1]
    npair = pair_live.shape[0]
    vmem = pl.BlockSpec(memory_space=pltpu.VMEM)
    f32 = jnp.float32
    polar = polarizability.reshape(1, nloc)
    tensors = pltpu.VMEM((NBLK * NGRP * 9, GROUP, BLOCK), f32)
    steps = len(OFFSETS)
    basis, gram = pl.pallas_call(
        functools.partial(field_kernel, sizes),
        out_shape=(
            jax.ShapeDtypeStruct((32, nloc), f32),
            jax.ShapeDtypeStruct((16, BLOCK), f32),
        ),
        in_specs=[vmem] * 9,
        out_specs=(vmem, vmem),
        scratch_shapes=[
            pltpu.VMEM((3, CX, CY, 8, BLOCK), f32),
            pltpu.VMEM((3, CX, CY, 4, BLOCK), f32),
            pltpu.VMEM((3, CX, CY, 4, BLOCK), f32),
            pltpu.VMEM((2, 3, 16, BLOCK), f32),
            pltpu.VMEM((2, 24, BLOCK), f32),
            pltpu.VMEM((2, 16, BLOCK), f32),
            pltpu.VMEM((2, 24, BLOCK), f32),
            pltpu.SemaphoreType.DMA((3, steps)),
            pltpu.SemaphoreType.DMA((3, steps)),
            pltpu.SemaphoreType.DMA((8,)),
            pltpu.SemaphoreType.DMA((8,)),
            pltpu.VMEM((NBLK, BLOCK, BLOCK), f32),
            pltpu.VMEM((NBLK, 8, BLOCK), f32),
            pltpu.VMEM((NBLK * NGRP, GROUP, 8), f32),
            pltpu.VMEM((NCOL * NGRP, 8, BLOCK), f32),
            pltpu.VMEM((NCOL * NGRP, 4, BLOCK), f32),
            pltpu.VMEM((3, NCOL, BLOCK), f32),
            tensors, tensors, tensors, tensors,
            pltpu.VMEM((NBLK, 3, BLOCK, BLOCK), f32),
            pltpu.VMEM((4, NBLK, 8, BLOCK), f32),
        ],
        compiler_params=pltpu.CompilerParams(
            collective_id=0, has_side_effects=True, vmem_limit_bytes=48 * 2**20
        ),
    )(
        coords, polar, external_field, bead_live.reshape(1, nloc),
        ghost_x, ghost_y, ghost_z, pair_blocks, pair_live.reshape(1, npair),
    )
    return pl.pallas_call(
        functools.partial(reduce_kernel, sizes),
        out_shape=(
            jax.ShapeDtypeStruct((3, nloc), f32),
            jax.ShapeDtypeStruct((3, nloc), f32),
        ),
        in_specs=[vmem] * 3,
        out_specs=(vmem, vmem),
        scratch_shapes=[pltpu.VMEM((n, 16, BLOCK), f32) for n in sizes]
        + [pltpu.SemaphoreType.DMA((n - 1,)) for n in sizes] * 2,
        compiler_params=pltpu.CompilerParams(collective_id=1, has_side_effects=True),
    )(basis, gram, polar)


def solution(mesh):
    sizes = tuple(mesh.shape[name] for name in ("gx", "gy", "gz"))
    wide = P(None, ("gx", "gy", "gz"))
    flat = P(("gx", "gy", "gz"))
    return jax.shard_map(
        functools.partial(per_device, sizes),
        mesh=mesh,
        in_specs=(wide, flat, wide, flat, wide, wide, wide, wide, flat),
        out_specs=(wide, wide),
        check_vma=False,
    )
```

time: 1130 us -> 94.5 us (0.08)
  blocking collectives: 640 us -> 0 us
  local copies, waits for them, and re-layouts: 248 us -> 8.77 us
  other arithmetic: 142 us -> 0 us
  Pallas kernels: 0 us -> 84.5 us
  starting transfers between devices: 68.8 us -> 0 us
    psum x5 -> x0, blocking collectives: 640 us -> none  [the longest x3 345 us: global_sum(): return lax.psum(value, ('gx', 'gy', 'gz'))]
    gather x189 -> x0, local copies, waits for them, and re-layouts: 191 us -> none  [the longest x8 81.2 us: spread(): jnp.take(ghosted, ghost_z[slot_index], axis=1)]
    reduce_sum x56 -> x0, other arithmetic: 88.7 us -> none  [the longest x51 85.6 us: pair_field(): field_x = jnp.sum(outer * along * delta_x - inner * moment_x, axis=2)]
    pallas_call x0 -> x2, Pallas kernels: none -> 84.5 us  [the longest x1 60.6 us: per_device(): pl.pallas_call(functools.partial(field_kernel, sizes), out_shape=(jax.Sha...]
    ppermute x24 -> x0, starting transfers between devices: 68.8 us -> none  [passed_along(): return lax.ppermute(value, axis, pairs)]
    select_n x232 -> x0, other arithmetic: 36.9 us -> none  [the longest x8 17.8 us: spread(): jnp.take(ghosted, ghost_z[slot_index], axis=1)]
    dynamic_slice x51 -> x0, local copies, waits for them, and re-layouts: 15.6 us -> none  [accumulate(): weight_row = lax.dynamic_slice_in_dim(weights, start, count)]
  transfers between devices with their start and end apart: 24 -> 0, of which waited for: 6 -> 0; matrix products, arithmetic and copies ran while one was open for 10% -> 0% of each run, Pallas kernels for 0% -> 0%
where the time goes in v1:
time: 94.5 us; the launch traced here: 94 us
  Pallas kernels  84.5 us (89%)
  local copies, waits for them, and re-layouts  8.77 us (9%)
    pallas_call x1, Pallas kernels, per_device(): pl.pallas_call(functools.partial(field_kernel, sizes), out_shape=(jax.Sha...  60.6 us
    pallas_call x1, Pallas kernels, per_device(): pl.pallas_call(functools.partial(reduce_kernel, sizes), out_shape=(jax.Sh...  23.9 us
    unnamed x26, local copies, waits for them, and re-layouts  8.77 us

profile of v1, /device:TPU:1, one launch (start us, length us, event | category | flops | bytes accessed | tf_op | source)
XLA Modules:
  0.0 94.0 jit_solution(15075848860198239447)
XLA Ops:
  0.6 0.0 copy-start.4
  0.6 0.0 copy-start.10
  0.7 0.7 copy-done.4
  1.3 0.0 copy-done.10
  1.3 0.0 copy-start.1
  1.3 0.7 copy-done.1
  2.1 0.0 copy-start.2
  2.1 0.7 copy-done.2
  2.8 0.0 copy-start.3
  2.8 0.7 copy-done.3
  3.5 0.0 copy-start.6
  3.5 0.7 copy-done.6
  4.2 0.7 copy-done.7
  4.9 0.7 copy-done.8
  5.6 0.7 copy-done.9
  6.2 60.6 %shard_map.104 = (f32[32,1024]{1,0:T(8,128)S(1)}, f32[16,128]{1,0:T(8,128)S(1)}) custom-call(f32[3,1024]{1,0:T(4,128)S(1)} %copy-done.2, f32[1,1024]{1,0:T(1,128)S(1)} %bitcast.4, f32[3,1024]{1,0:T(4,128)S(1)} %copy-done.3, s32[1,1024]{1,0:T(1,128)S(1)} %bitcast.5, s32[2,256]{1,0:T(2,128)S(1)} %copy-done.8, s32[2,768]{1,0:T(2,128)S(1)} %copy-done.6, ...), custom_call_target="tpu_custom_call" | custom-call | tf_op jit(solution)/shard_map/pallas_call | solution.py:508
  66.9 0.0 copy-start
  66.9 0.6 copy-done
  67.5 0.6 copy-done.5
  68.1 23.9 %shard_map.105 = (f32[3,1024]{1,0:T(4,128)}, f32[3,1024]{1,0:T(4,128)}) custom-call(f32[32,1024]{1,0:T(8,128)} %copy-done, f32[16,128]{1,0:T(8,128)} %copy-done.5, f32[1,1024]{1,0:T(1,128)} %bitcast.3), custom_call_target="tpu_custom_call" | custom-call | tf_op jit(solution)/shard_map/pallas_call | solution.py:545
  92.0 0.0 copy-start.11
  92.0 1.3 %copy.13 = f32[3,1024]{1,0:T(4,128)} copy(f32[3,1024]{1,0:T(4,128)} %get-tuple-element.8) | data formatting | bytes 24576
  93.4 0.0 copy-done.11
  93.4 0.6 copy.14
  (4 shorter events, 0.0 us)
Async XLA Ops:
  0.6 0.7 copy-start.4
  0.6 0.7 copy-start.10
  1.3 0.7 copy-start.1
  2.1 0.7 copy-start.2
  2.8 0.7 copy-start.3
  3.5 0.7 copy-start.6
  4.2 0.7 copy-start.7
  4.9 0.7 copy-start.8
  5.6 0.7 copy-start.9
  66.9 0.7 copy-start
  67.5 0.6 copy-start.5
  92.0 1.3 %copy-start.11 = (f32[3,1024]{1,0:T(4,128)S(1)}, f32[3,1024]{1,0:T(4,128)}, u32[]{:S(2)}) copy-start(f32[3,1024]{1,0:T(4,128)} %get-tuple-element.9) | copy-start | bytes 36868

commit v2 on v1

--- a/solution.py
+++ b/solution.py
@@ -133,15 +133,108 @@
     return copies
 
 
+def partners_of(me, sizes):
+    steps = []
+    for axis, n in enumerate(sizes):
+        for s in range(1, n):
+            step = [0, 0, 0]
+            step[axis] = s if 2 * s <= n else s - n
+            steps.append(tuple(step))
+    return steps
+
+
+def reduce_along(axis, n, total, slot, send, recv, me, sizes):
+    slot[me[axis]] = total
+    copies = []
+    for s in range(1, n):
+        step = [0, 0, 0]
+        step[axis] = s
+        copies.append(
+            pltpu.make_async_remote_copy(
+                src_ref=slot.at[me[axis]],
+                dst_ref=slot.at[me[axis]],
+                send_sem=send.at[s - 1],
+                recv_sem=recv.at[s - 1],
+                device_id=neighbour(me, sizes, step),
+                device_id_type=MESH,
+            )
+        )
+    for copy in copies:
+        copy.start()
+    for copy in copies:
+        copy.wait_recv()
+    total = slot[0]
+    for k in range(1, n):
+        total = total + slot[k]
+    return total, copies
+
+
+def gradient_steps(products):
+    def inner(left, right):
+        value = 0.0
+        for a, p in enumerate(left):
+            for b, q in enumerate(right):
+                if p is not None and q is not None:
+                    value = value + p * q * products[a, b]
+        return value
+
+    def plus(p, q):
+        return q if p is None else (p if q is None else p + q)
+
+    def times(scale, p):
+        return None if p is None else scale * p
+
+    def applied(c):
+        out = [times(CENTRE, p) for p in c]
+        if c[0] is not None:
+            out[1] = plus(out[1], HALF * c[0])
+        for k in (1, 2):
+            if c[k] is not None:
+                out[k - 1] = plus(out[k - 1], (0.5 * HALF) * c[k])
+                out[k + 1] = plus(out[k + 1], (0.5 * HALF) * c[k])
+        return out
+
+    left = [jnp.ones((1, 1), jnp.float32), None, None, None]
+    direction = list(left)
+    answer = [None] * 4
+    norm = products[0, 0]
+    for _ in range(3):
+        image = applied(direction)
+        step = norm / inner(direction, image)
+        answer = [plus(p, times(step, q)) for p, q in zip(answer, direction)]
+        left = [plus(p, times(-step, q)) for p, q in zip(left, image)]
+        after = inner(left, left)
+        direction = [plus(p, times(after / norm, q)) for p, q in zip(left, direction)]
+        norm = after
+    return answer, left
+
+
 def field_kernel(
     sizes,
-    coords, polar, external, live, ghost_x, ghost_y, ghost_z, pairs, alive,
-    basis_out, gram_out,
+    coords_in, polar_in, external_in, live_in, ghost_x_in, ghost_y_in, ghost_z_in,
+    pairs_in, alive_in,
+    dipoles, residual,
+    coords, polar, external, live, ghost_x, ghost_y, ghost_z, pairs, alive, loads,
     halo1, halo2, halo3, tabs_y, tabs_z, own_y, own_z, sends, recvs, tab_sends, tab_recvs,
-    order, side, target, window, moved, marks, px, py, pz, inner_s, sums, basis,
+    order, side, target, window, moved, marks, px, py, pz, inner_s, sums, basis, flat,
+    slot_x, slot_y, slot_z, send_x, send_y, send_z, recv_x, recv_y, recv_z,
 ):
     me = place_of(sizes)
-    barrier = greet([neighbour(me, sizes, step) for step in OFFSETS])
+    outside = (
+        coords_in, polar_in, external_in, live_in, ghost_x_in, ghost_y_in, ghost_z_in,
+        pairs_in, alive_in,
+    )
+    inside = (coords, polar, external, live, ghost_x, ghost_y, ghost_z, pairs, alive)
+    arriving = [
+        pltpu.make_async_copy(far, near, loads.at[n])
+        for n, (far, near) in enumerate(zip(outside, inside))
+    ]
+    for copy in arriving:
+        copy.start()
+    friends = dict.fromkeys(list(OFFSETS) + partners_of(me, sizes))
+    barrier = greet([neighbour(me, sizes, step) for step in friends])
+    for copy in arriving:
+        copy.wait()
 
     up_blocks, up_lanes = inverse_list(ghost_x, 0, 0, 2 * BLOCK, NBLK)
     down_blocks, down_lanes = inverse_list(ghost_x, 1, 0, 2 * BLOCK, NBLK)
@@ -185,7 +278,7 @@
         for g in range(NGRP):
             target[b * NGRP + g] = flipped[g * GROUP : (g + 1) * GROUP]
 
-    pl.semaphore_wait(barrier, len(OFFSETS))
+    pl.semaphore_wait(barrier, len(friends))
     first = halo_copies(halo1, sends.at[0], recvs.at[0], me, sizes)
     for copy in first:
         copy.start()
@@ -393,105 +486,34 @@
     for a, b in GRAM:
         part = jnp.sum(basis[a] * basis[b], axis=0)
         rows.append(jnp.sum(part, axis=0, keepdims=True))
-    rows.append(jnp.zeros((16 - len(GRAM), BLOCK), jnp.float32))
-    gram_out[...] = jnp.concatenate(rows, axis=0)
-    for b in range(NBLK):
-        stacked = jnp.concatenate([basis[k, b] for k in range(4)], axis=0)
-        basis_out[:, b * BLOCK : (b + 1) * BLOCK] = dot_lanes(stacked, order[b])
-    for copy in started:
-        copy.wait_send()
-
-
-def reduce_kernel(sizes, basis, gram, polar, dipoles, residual, *scratch):
-    slots, send_sems, recv_sems = scratch[0:3], scratch[3:6], scratch[6:9]
-    me = place_of(sizes)
-    partners = []
+    rows.append(jnp.zeros((BLOCK - len(GRAM), BLOCK), jnp.float32))
+    total = dot_lanes(ones, jnp.concatenate(rows, axis=0))[0:1]
+    slots, sent, got = (slot_x, slot_y, slot_z), (send_x, send_y, send_z), (recv_x, recv_y, recv_z)
     for axis, n in enumerate(sizes):
-        for s in range(1, n):
-            step = [0, 0, 0]
-            step[axis] = s
-            partners.append(neighbour(me, sizes, step))
-    barrier = greet(partners)
-    total = gram[...]
-    for axis, n in enumerate(sizes):
-        slot, send, recv = slots[axis], send_sems[axis], recv_sems[axis]
-        slot[me[axis]] = total
+        total, copies = reduce_along(
+            axis, n, total, slots[axis], sent[axis], got[axis], me, sizes
+        )
+        started = started + copies
         if axis == 0:
-            pl.semaphore_wait(barrier, len(partners))
-        copies = []
-        for s in range(1, n):
-            step = [0, 0, 0]
-            step[axis] = s
-            copies.append(
-                pltpu.make_async_remote_copy(
-                    src_ref=slot.at[me[axis]],
-                    dst_ref=slot.at[me[axis]],
-                    send_sem=send.at[s - 1],
-                    recv_sem=recv.at[s - 1],
-                    device_id=neighbour(me, sizes, step),
-                    device_id_type=MESH,
-                )
-            )
-        for copy in copies:
-            copy.start()
-        for copy in copies:
-            copy.wait()
-        total = slot[0]
-        for k in range(1, n):
-            total = total + slot[k]
-
-    whole = jnp.sum(total, axis=1, keepdims=True)
+            for b in range(NBLK):
+                stacked = jnp.concatenate([basis[k, b] for k in range(4)], axis=0)
+                flat[:, b * BLOCK : (b + 1) * BLOCK] = dot_lanes(stacked, order[b])
     products = {}
     for k, (a, b) in enumerate(GRAM):
-        products[a, b] = products[b, a] = whole[k : k + 1, :]
-
-    def inner(left, right):
-        value = 0.0
-        for a, p in enumerate(left):
-            for b, q in enumerate(right):
-                if p is not None and q is not None:
-                    value = value + p * q * products[a, b]
-        return value
-
-    def plus(p, q):
-        return q if p is None else (p if q is None else p + q)
-
-    def times(scale, p):
-        return None if p is None else scale * p
-
-    def applied(c):
-        out = [times(CENTRE, p) for p in c]
-        if c[0] is not None:
-            out[1] = plus(out[1], HALF * c[0])
-        for k in (1, 2):
-            if c[k] is not None:
-                out[k - 1] = plus(out[k - 1], (0.5 * HALF) * c[k])
-                out[k + 1] = plus(out[k + 1], (0.5 * HALF) * c[k])
-        return out
-
-    one = jnp.ones((1, 1), jnp.float32)
-    left = [one, None, None, None]
-    direction = list(left)
-    answer = [None] * 4
-    norm = products[0, 0]
-    for _ in range(3):
-        image = applied(direction)
-        step = norm / inner(direction, image)
-        answer = [plus(p, times(step, q)) for p, q in zip(answer, direction)]
-        left = [plus(p, times(-step, q)) for p, q in zip(left, image)]
-        after = inner(left, left)
-        direction = [plus(p, times(after / norm, q)) for p, q in zip(left, direction)]
-        norm = after
+        products[a, b] = products[b, a] = total[:, k : k + 1]
+    answer, left = gradient_steps(products)
 
     def combined(coefficients):
         value = 0.0
         for k, c in enumerate(coefficients):
             if c is not None:
-                value = value + c * basis[8 * k : 8 * k + 3, :]
+                value = value + c * flat[8 * k : 8 * k + 3, :]
         return value
 
     dipoles[...] = combined(answer)
     residual[...] = polar[...] * combined(left)
+    for copy in started:
+        copy.wait_send()
 
 
 def per_device(
@@ -499,21 +521,22 @@
     ghost_x, ghost_y, ghost_z, pair_blocks, pair_live,
 ):
     nloc = coords.shape[1]
-    npair = pair_live.shape[0]
     vmem = pl.BlockSpec(memory_space=pltpu.VMEM)
     f32 = jnp.float32
-    polar = polarizability.reshape(1, nloc)
+    operands = (
+        coords, polarizability.reshape(1, nloc), external_field, bead_live.reshape(1, nloc),
+        ghost_x, ghost_y, ghost_z, pair_blocks, pair_live.reshape(1, pair_live.shape[0]),
+    )
     tensors = pltpu.VMEM((NBLK * NGRP * 9, GROUP, BLOCK), f32)
     steps = len(OFFSETS)
-    basis, gram = pl.pallas_call(
+    return pl.pallas_call(
         functools.partial(field_kernel, sizes),
-        out_shape=(
-            jax.ShapeDtypeStruct((32, nloc), f32),
-            jax.ShapeDtypeStruct((16, BLOCK), f32),
-        ),
-        in_specs=[vmem] * 9,
+        out_shape=(jax.ShapeDtypeStruct((3, nloc), f32),) * 2,
+        in_specs=[pl.BlockSpec(memory_space=pl.ANY)] * len(operands),
         out_specs=(vmem, vmem),
-        scratch_shapes=[
+        scratch_shapes=[pltpu.VMEM(x.shape, x.dtype) for x in operands]
+        + [
+            pltpu.SemaphoreType.DMA((len(operands),)),
             pltpu.VMEM((3, CX, CY, 8, BLOCK), f32),
             pltpu.VMEM((3, CX, CY, 4, BLOCK), f32),
             pltpu.VMEM((3, CX, CY, 4, BLOCK), f32),
@@ -534,26 +557,14 @@
             tensors, tensors, tensors, tensors,
             pltpu.VMEM((NBLK, 3, BLOCK, BLOCK), f32),
             pltpu.VMEM((4, NBLK, 8, BLOCK), f32),
-        ],
+            pltpu.VMEM((32, nloc), f32),
+        ]
+        + [pltpu.VMEM((n, 1, BLOCK), f32) for n in sizes]
+        + [pltpu.SemaphoreType.DMA((n - 1,)) for n in sizes] * 2,
         compiler_params=pltpu.CompilerParams(
             collective_id=0, has_side_effects=True, vmem_limit_bytes=48 * 2**20
         ),
-    )(
-        coords, polar, external_field, bead_live.reshape(1, nloc),
-        ghost_x, ghost_y, ghost_z, pair_blocks, pair_live.reshape(1, npair),
-    )
-    return pl.pallas_call(
-        functools.partial(reduce_kernel, sizes),
-        out_shape=(
-            jax.ShapeDtypeStruct((3, nloc), f32),
-            jax.ShapeDtypeStruct((3, nloc), f32),
-        ),
-        in_specs=[vmem] * 3,
-        out_specs=(vmem, vmem),
-        scratch_shapes=[pltpu.VMEM((n, 16, BLOCK), f32) for n in sizes]
-        + [pltpu.SemaphoreType.DMA((n - 1,)) for n in sizes] * 2,
-        compiler_params=pltpu.CompilerParams(collective_id=1, has_side_effects=True),
-    )(basis, gram, polar)
+    )(*operands)
 
 
 def solution(mesh):

time: 94.5 us -> 83.3 us (0.88)
  Pallas kernels: 84.5 us -> 75.4 us
  local copies, waits for them, and re-layouts: 8.77 us -> 6.8 us
    pallas_call x1 -> x0, Pallas kernels: 23.9 us -> none  [per_device(): pl.pallas_call(functools.partial(reduce_kernel, sizes), out_shape=(jax.Sh...]
    pallas_call x1, Pallas kernels: 60.6 us -> 75.4 us  [per_device(): pl.pallas_call(functools.partial(field_kernel, sizes), out_shape=(jax.Sha...]
    unnamed x26 -> x20, local copies, waits for them, and re-layouts: 8.77 us -> 6.8 us
where the time goes in v2:
time: 83.3 us; the launch traced here: 82.9 us
  Pallas kernels  75.4 us (91%)
  local copies, waits for them, and re-layouts  6.8 us (8%)
    pallas_call x1, Pallas kernels, per_device(): pl.pallas_call(functools.partial(field_kernel, sizes), out_shape=(jax.Sha...  75.4 us
    unnamed x20, local copies, waits for them, and re-layouts  6.8 us

profile of v2, /device:TPU:1, one launch (start us, length us, event | category | flops | bytes accessed | tf_op | source)
XLA Modules:
  0.0 82.9 jit_solution(1595364039153344919)
XLA Ops:
  0.6 0.0 copy-start.4
  0.6 0.0 copy-start.8
  0.7 0.7 copy-done.4
  1.3 0.0 copy-done.8
  1.3 0.0 copy-start
  1.3 0.7 copy-done
  2.1 0.0 copy-start.1
  2.1 0.7 copy-done.1
  2.8 0.0 copy-start.2
  2.8 0.7 copy-done.2
  3.5 0.0 copy-start.3
  3.5 0.7 copy-done.3
  4.2 0.0 copy-start.5
  4.2 0.7 copy-done.5
  4.9 0.0 copy-start.6
  4.9 0.7 copy-done.6
  5.6 0.0 copy-start.7
  5.6 0.7 copy-done.7
  6.2 75.4 %shard_map.104 = (f32[3,1024]{1,0:T(4,128)S(1)}, f32[3,1024]{1,0:T(4,128)S(1)}) custom-call(f32[3,1024]{1,0:T(4,128)S(1)} %copy-done.1, f32[1,1024]{1,0:T(1,128)S(1)} %bitcast.3, f32[3,1024]{1,0:T(4,128)S(1)} %copy-done.2, s32[1,1024]{1,0:T(1,128)S(1)} %bitcast.4, s32[2,256]{1,0:T(2,128)S(1)} %copy-done.6, s32[2,768]{1,0:T(2,128)S(1)} %copy-done.3, ...), custom_call_target="tpu_custom_call" | custom-call | tf_op jit(solution)/shard_map/pallas_call | solution.py:532
  81.7 0.6 copy.13
  82.3 0.6 copy.14
Async XLA Ops:
  0.6 0.7 copy-start.4
  0.6 0.7 copy-start.8
  1.3 0.7 copy-start
  2.1 0.7 copy-start.1
  2.8 0.7 copy-start.2
  3.5 0.7 copy-start.3
  4.2 0.7 copy-start.5
  4.9 0.7 copy-start.6
  5.6 0.7 copy-start.7

commit v3 on v2

--- a/solution.py
+++ b/solution.py
@@ -46,6 +46,21 @@
     )
 
 
+def halves(x, parts):
+    out = []
+    for _ in range(parts):
+        part = x.astype(jnp.bfloat16)
+        out.append(part)
+        x = x - part.astype(jnp.float32)
+    return jnp.concatenate(out, axis=0)
+
+
+def permuted(dot, x, one_hot):
+    rows = x.shape[0]
+    out = dot(halves(x, 3), one_hot, None)
+    return out[:rows] + out[rows : 2 * rows] + out[2 * rows :]
+
+
 def iota(shape, axis):
     return lax.broadcasted_iota(jnp.int32, shape, axis)
 
@@ -216,7 +231,7 @@
     dipoles, residual,
     coords, polar, external, live, ghost_x, ghost_y, ghost_z, pairs, alive, loads,
     halo1, halo2, halo3, tabs_y, tabs_z, own_y, own_z, sends, recvs, tab_sends, tab_recvs,
-    order, side, target, window, moved, marks, px, py, pz, inner_s, sums, basis, flat,
+    order, side, target, window, listed_bits, moved, marks, px, py, pz, inner_s, sums, basis, flat,
     slot_x, slot_y, slot_z, send_x, send_y, send_z, recv_x, recv_y, recv_z,
 ):
     me = place_of(sizes)
@@ -267,8 +282,9 @@
         )
         rank = jnp.sum(before.astype(jnp.float32), axis=1, keepdims=True)
         one_hot = (rank == iota((BLOCK, BLOCK), 1).astype(jnp.float32)).astype(jnp.float32)
+        one_hot = one_hot.astype(jnp.bfloat16)
         order[b] = one_hot
-        ranked = dot_rows(jnp.concatenate([tile, more], axis=0), one_hot)
+        ranked = permuted(dot_rows, jnp.concatenate([tile, more], axis=0), one_hot)
         halo1[1, 1 + b // NBY, 1 + b % NBY] = ranked[:8]
         side[b] = ranked[8:]
         basis[0, b] = jnp.concatenate(
@@ -389,43 +405,60 @@
         for cy in range(CY):
             tiles = windows(*[shifted(role, cx, cy) for role in range(3)], lane8)
             for g in range(NGRP):
-                window[(cx * CY + cy) * NGRP + g] = tiles[g]
+                for k in range(7):
+                    window[(cx * CY + cy) * NGRP + g, k] = jnp.broadcast_to(
+                        tiles[g][k : k + 1], (8, BLOCK)
+                    )
+                listed_bits[(cx * CY + cy) * NGRP + g] = jnp.broadcast_to(
+                    tiles[g][7:8], (8, BLOCK)
+                ).astype(jnp.int32)
+
+    tiles_of = (GROUP // 8, 8, BLOCK)
+
+    def keep_sums(block, g, total):
+        for k in range(3):
+            sums[block, k, pl.ds(pl.multiple_of(g * GROUP, GROUP), GROUP)] = total[k].reshape(
+                GROUP, BLOCK
+            )
 
     def build(step, carry):
         block, g = step // NGRP, step % NGRP
         column = (block // NBY) * CY + block % NBY
         mine = target[step]
-        tx, ty, tz, tb = [jnp.broadcast_to(mine[:, k : k + 1], (GROUP, BLOCK)) for k in range(4)]
-        total = [jnp.zeros((GROUP, BLOCK), jnp.float32) for _ in range(3)]
+        tx, ty, tz, tb = [
+            jnp.broadcast_to(mine[:, k : k + 1], (GROUP, BLOCK)).reshape(tiles_of)
+            for k in range(4)
+        ]
+        total = [jnp.zeros(tiles_of, jnp.float32) for _ in range(3)]
+        bit = jnp.left_shift(1, block)
         for c in range(9):
-            tile = window[(column + (c // 3) * CY + c % 3) * NGRP + g]
-            bit = jnp.right_shift(tile[7:8].astype(jnp.int32), block)
-            seen = jnp.bitwise_and(bit, 1) == 1
-            sx = jnp.where(seen, tile[0:1], FAR)
-            dx, dy, dz = tx - sx, ty - tile[1:2], tz - tile[2:3]
+            at = (column + (c // 3) * CY + c % 3) * NGRP + g
+            seen = jnp.bitwise_and(listed_bits[at], bit) != 0
+            sx = jnp.where(seen, window[at, 0], FAR)
+            dx, dy, dz = tx - sx[None], ty - window[at, 1][None], tz - window[at, 2][None]
             if c == 4:
-                itself = iota((GROUP, BLOCK), 0) + g * GROUP == iota((GROUP, BLOCK), 1)
-                dx = jnp.where(itself, FAR, dx)
+                mine_at = iota(tiles_of, 0) * 8 + iota(tiles_of, 1) + g * GROUP
+                dx = jnp.where(mine_at == iota(tiles_of, 2), FAR, dx)
             q = dx * dx + dy * dy + dz * dz
             inv = lax.rsqrt(q)
             inv2 = inv * inv
-            margin = jnp.maximum(1.0 - q * (1.0 / CUTOFF_SQUARED), 0.0)
-            scaled = q * (q * inv) * (tb * tile[3:4])
+            margin = jnp.maximum(CUTOFF_SQUARED - q, 0.0)
+            scaled = q * (q * inv) * (tb * window[at, 3][None])
             damp = jnp.exp(-scaled)
             rest = 1.0 - damp
-            inner = (margin * margin) * (inv2 * inv) * rest
-            root = (3.0 * inv) * jnp.maximum(rest - scaled * damp, 1e-20)
-            scale = margin * inv2 * root * lax.rsqrt(root)
+            near = margin * inv2
+            inner = (near * margin) * (inv * rest)
+            root = (3.0 * inv) * (rest - scaled * damp)
+            scale = near * (root * lax.rsqrt(root))
             ax, ay, az = scale * dx, scale * dy, scale * dz
             slot = step * 9 + c
             px[slot], py[slot], pz[slot], inner_s[slot] = ax, ay, az, inner
-            vx, vy, vz = tile[4:5], tile[5:6], tile[6:7]
+            vx, vy, vz = window[at, 4][None], window[at, 5][None], window[at, 6][None]
             along = ax * vx + ay * vy + az * vz
             total[0] = total[0] + (along * ax - inner * vx)
             total[1] = total[1] + (along * ay - inner * vy)
             total[2] = total[2] + (along * az - inner * vz)
-        for k in range(3):
-            sums[block, k, pl.ds(pl.multiple_of(g * GROUP, GROUP), GROUP)] = total[k]
+        keep_sums(block, g, total)
         return carry
 
     lax.fori_loop(0, NBLK * NGRP, build, 0)
@@ -433,26 +466,33 @@
     def apply(step, carry):
         block, g = step // NGRP, step % NGRP
         column = (block // NBY) * CY + block % NBY
-        total = [jnp.zeros((GROUP, BLOCK), jnp.float32) for _ in range(3)]
+        total = [jnp.zeros(tiles_of, jnp.float32) for _ in range(3)]
         for c in range(9):
-            tile = moved[(column + (c // 3) * CY + c % 3) * NGRP + g]
+            at = (column + (c // 3) * CY + c % 3) * NGRP + g
             slot = step * 9 + c
             ax, ay, az, inner = px[slot], py[slot], pz[slot], inner_s[slot]
-            vx, vy, vz = tile[0:1], tile[1:2], tile[2:3]
+            vx, vy, vz = moved[at, 0][None], moved[at, 1][None], moved[at, 2][None]
             along = ax * vx + ay * vy + az * vz
             total[0] = total[0] + (along * ax - inner * vx)
             total[1] = total[1] + (along * ay - inner * vy)
             total[2] = total[2] + (along * az - inner * vz)
-        for k in range(3):
-            sums[block, k, pl.ds(pl.multiple_of(g * GROUP, GROUP), GROUP)] = total[k]
+        keep_sums(block, g, total)
         return carry
 
     ones = jnp.ones((8, BLOCK), jnp.float32)
+    ones_half = ones.astype(jnp.bfloat16)
 
     def next_basis(level, halo):
         for b in range(NBLK):
-            field = [dot_lanes(ones, sums[b, k]) for k in range(3)]
+            parts = [halves(sums[b, k], 2) for k in range(3)]
+            field = dot_lanes(ones_half, jnp.concatenate(parts, axis=0), None)
+            field = [
+                field[:, 2 * k * BLOCK : (2 * k + 1) * BLOCK]
+                + field[:, (2 * k + 1) * BLOCK : (2 * k + 2) * BLOCK]
+                for k in range(3)
+            ]
             field = jnp.where(row8 == 0, field[0], jnp.where(row8 == 1, field[1], field[2]))
+            field = field * (1.0 / CUTOFF_SQUARED**2)
             v = basis[level, b]
             rows = side[b]
             image = rows[0:1] * v - rows[1:2] * field
@@ -477,7 +517,10 @@
             for cy in range(CY):
                 tiles = windows(*[halo[role, cx, cy] for role in range(3)], lane4)
                 for g in range(NGRP):
-                    moved[(cx * CY + cy) * NGRP + g] = tiles[g]
+                    for k in range(3):
+                        moved[(cx * CY + cy) * NGRP + g, k] = jnp.broadcast_to(
+                            tiles[g][k : k + 1], (8, BLOCK)
+                        )
         lax.fori_loop(0, NBLK * NGRP, apply, 0)
         started = started + copies
     next_basis(2, None)
@@ -497,7 +540,7 @@
         if axis == 0:
             for b in range(NBLK):
                 stacked = jnp.concatenate([basis[k, b] for k in range(4)], axis=0)
-                flat[:, b * BLOCK : (b + 1) * BLOCK] = dot_lanes(stacked, order[b])
+                flat[:, b * BLOCK : (b + 1) * BLOCK] = permuted(dot_lanes, stacked, order[b])
     products = {}
     for k, (a, b) in enumerate(GRAM):
         products[a, b] = products[b, a] = total[:, k : k + 1]
@@ -527,12 +570,12 @@
         coords, polarizability.reshape(1, nloc), external_field, bead_live.reshape(1, nloc),
         ghost_x, ghost_y, ghost_z, pair_blocks, pair_live.reshape(1, pair_live.shape[0]),
     )
-    tensors = pltpu.VMEM((NBLK * NGRP * 9, GROUP, BLOCK), f32)
+    tensors = pltpu.VMEM((NBLK * NGRP * 9, GROUP // 8, 8, BLOCK), f32)
     steps = len(OFFSETS)
     return pl.pallas_call(
         functools.partial(field_kernel, sizes),
         out_shape=(jax.ShapeDtypeStruct((3, nloc), f32),) * 2,
-        in_specs=[pl.BlockSpec(memory_space=pl.ANY)] * len(operands),
+        in_specs=[pl.BlockSpec(memory_space=pltpu.HBM)] * len(operands),
         out_specs=(vmem, vmem),
         scratch_shapes=[pltpu.VMEM(x.shape, x.dtype) for x in operands]
         + [
@@ -548,11 +591,12 @@
             pltpu.SemaphoreType.DMA((3, steps)),
             pltpu.SemaphoreType.DMA((8,)),
             pltpu.SemaphoreType.DMA((8,)),
-            pltpu.VMEM((NBLK, BLOCK, BLOCK), f32),
+            pltpu.VMEM((NBLK, BLOCK, BLOCK), jnp.bfloat16),
             pltpu.VMEM((NBLK, 8, BLOCK), f32),
             pltpu.VMEM((NBLK * NGRP, GROUP, 8), f32),
-            pltpu.VMEM((NCOL * NGRP, 8, BLOCK), f32),
-            pltpu.VMEM((NCOL * NGRP, 4, BLOCK), f32),
+            pltpu.VMEM((NCOL * NGRP, 7, 8, BLOCK), f32),
+            pltpu.VMEM((NCOL * NGRP, 8, BLOCK), jnp.int32),
+            pltpu.VMEM((NCOL * NGRP, 3, 8, BLOCK), f32),
             pltpu.VMEM((3, NCOL, BLOCK), f32),
             tensors, tensors, tensors, tensors,
             pltpu.VMEM((NBLK, 3, BLOCK, BLOCK), f32),
@@ -562,7 +606,7 @@
         + [pltpu.VMEM((n, 1, BLOCK), f32) for n in sizes]
         + [pltpu.SemaphoreType.DMA((n - 1,)) for n in sizes] * 2,
         compiler_params=pltpu.CompilerParams(
-            collective_id=0, has_side_effects=True, vmem_limit_bytes=48 * 2**20
+            collective_id=0, has_side_effects=True, vmem_limit_bytes=63 * 2**20
         ),
     )(*operands)
 

time: 83.3 us -> 72.2 us (0.87)
  Pallas kernels: 75.4 us -> 69.4 us
  local copies, waits for them, and re-layouts: 6.8 us -> 1.94 us
    pallas_call x1, Pallas kernels: 75.4 us -> 69.4 us  [per_device(): pl.pallas_call(functools.partial(field_kernel, sizes), out_shape=(jax.Sha...]
    unnamed x20 -> x4, local copies, waits for them, and re-layouts: 6.8 us -> 1.94 us
where the time goes in v3:
time: 72.2 us; the launch traced here: 72 us
  Pallas kernels  69.4 us (96%)
  local copies, waits for them, and re-layouts  1.94 us (3%)
    pallas_call x1, Pallas kernels, per_device(): pl.pallas_call(functools.partial(field_kernel, sizes), out_shape=(jax.Sha...  69.4 us
    unnamed x4, local copies, waits for them, and re-layouts  1.94 us

profile of v3, /device:TPU:1, one launch (start us, length us, event | category | flops | bytes accessed | tf_op | source)
XLA Modules:
  0.0 72.0 jit_solution(2858927706166304574)
XLA Ops:
  0.6 69.4 %shard_map.104 = (f32[3,1024]{1,0:T(4,128)}, f32[3,1024]{1,0:T(4,128)}) custom-call(f32[3,1024]{1,0:T(4,128)} %coords_in.1, f32[1,1024]{1,0:T(1,128)} %bitcast.3, f32[3,1024]{1,0:T(4,128)} %external_in.1, s32[1,1024]{1,0:T(1,128)} %bitcast.4, s32[2,256]{1,0:T(2,128)} %ghost_x_in.1, s32[2,768]{1,0:T(2,128)} %ghost_y_in.1, s32[2,3072]{1,0:T(2,128)} %ghost_z_in.1, ...), custom_call_target="tpu_custom_call" | custom-call | tf_op jit(solution)/shard_map/pallas_call | solution.py:575
  70.0 0.0 copy-start
  70.0 1.3 %copy.13 = f32[3,1024]{1,0:T(4,128)} copy(f32[3,1024]{1,0:T(4,128)} %get-tuple-element.4) | data formatting | bytes 24576
  71.4 0.0 copy-done
  71.4 0.6 copy.14
Async XLA Ops:
  70.0 1.3 %copy-start = (f32[3,1024]{1,0:T(4,128)S(1)}, f32[3,1024]{1,0:T(4,128)}, u32[]{:S(2)}) copy-start(f32[3,1024]{1,0:T(4,128)} %get-tuple-element.5) | copy-start | bytes 36868

commit v4 on v3

--- a/solution.py
+++ b/solution.py
@@ -73,6 +73,29 @@
     return (1, count) if step == 0 else ((0, 1) if step > 0 else (count + 1, 1))
 
 
+def site_ranks(place):
+    tie = iota((BLOCK, BLOCK), 0) < iota((BLOCK, BLOCK), 1)
+    base = jnp.zeros((NBLK, BLOCK), jnp.float32)
+    for axis, shift in ((2, 4), (0, 2), (1, 0)):
+        key = base + place[axis]
+        column = jnp.transpose(key)
+        ranks = []
+        for b in range(NBLK):
+            left = jnp.broadcast_to(column[:, b : b + 1], (BLOCK, BLOCK))
+            right = jnp.broadcast_to(key[b : b + 1, :], (BLOCK, BLOCK))
+            before = jnp.logical_or(left < right, jnp.logical_and(left == right, tie))
+            ranks.append(jnp.sum(jnp.where(before, 1.0, 0.0), axis=0, keepdims=True))
+        rank = jnp.concatenate(ranks, axis=0).astype(jnp.int32)
+        base = jnp.right_shift(rank, shift).astype(jnp.float32) * 512.0
+    return rank
+
+
+def site_lanes(rank):
+    z, x, y = jnp.right_shift(rank, 4), jnp.right_shift(rank, 2) & 3, rank & 3
+    cube = jnp.right_shift(z, 1) * 4 + jnp.right_shift(x, 1) * 2 + jnp.right_shift(y, 1)
+    return cube * 8 + (z & 1) * 4 + (x & 1) * 2 + (y & 1)
+
+
 def inverse_list(list_ref, row, first, entries, tables):
     blocks = jnp.zeros((tables, BLOCK), jnp.float32)
     lanes = jnp.zeros((tables, BLOCK), jnp.float32)
@@ -130,17 +153,21 @@
     return barrier
 
 
+def bytes_of(view, sem):
+    return pltpu.make_async_copy(view, view, sem)
+
+
 def halo_copies(buffer, send_sem, recv_sem, me, sizes):
     copies = []
-    for n, step in enumerate(OFFSETS):
+    for step in OFFSETS:
         (xs, xn), (ys, yn) = own_span(step[0], NBX), own_span(step[1], NBY)
         (xd, _), (yd, _) = halo_span(step[0], NBX), halo_span(step[1], NBY)
         copies.append(
             pltpu.make_async_remote_copy(
                 src_ref=buffer.at[1, pl.ds(1 + xs, xn), pl.ds(1 + ys, yn)],
                 dst_ref=buffer.at[1 - step[2], pl.ds(xd, xn), pl.ds(yd, yn)],
-                send_sem=send_sem.at[n],
-                recv_sem=recv_sem.at[n],
+                send_sem=send_sem,
+                recv_sem=recv_sem,
                 device_id=neighbour(me, sizes, step),
                 device_id_type=MESH,
             )
@@ -148,40 +175,38 @@
     return copies
 
 
-def partners_of(me, sizes):
-    steps = []
-    for axis, n in enumerate(sizes):
-        for s in range(1, n):
-            step = [0, 0, 0]
-            step[axis] = s if 2 * s <= n else s - n
-            steps.append(tuple(step))
-    return steps
-
-
-def reduce_along(axis, n, total, slot, send, recv, me, sizes):
-    slot[me[axis]] = total
+def sum_stages(sizes):
+    def near(step):
+        return tuple(s if 2 * s <= n else s - n for s, n in zip(step, sizes))
+
+    along = [near((s, 0, 0)) for s in range(1, sizes[0])]
+    across = [near((0, y, z)) for y in range(sizes[1]) for z in range(sizes[2]) if y + z > 0]
+    far_first = lambda step: -sum(abs(s) for s in step)
+    return sorted(along, key=far_first), sorted(across, key=far_first)
+
+
+def reduce_over(steps, total, slot, place, send, recv, me, sizes):
+    slot[place] = total
     copies = []
-    for s in range(1, n):
-        step = [0, 0, 0]
-        step[axis] = s
+    for step in steps:
         copies.append(
             pltpu.make_async_remote_copy(
-                src_ref=slot.at[me[axis]],
-                dst_ref=slot.at[me[axis]],
-                send_sem=send.at[s - 1],
-                recv_sem=recv.at[s - 1],
+                src_ref=slot.at[place],
+                dst_ref=slot.at[place],
+                send_sem=send,
+                recv_sem=recv,
                 device_id=neighbour(me, sizes, step),
                 device_id_type=MESH,
             )
         )
     for copy in copies:
         copy.start()
-    for copy in copies:
-        copy.wait_recv()
+    everyone = slot.at[pl.ds(0, len(steps))]
+    bytes_of(everyone, recv).wait()
     total = slot[0]
-    for k in range(1, n):
+    for k in range(1, len(steps) + 1):
         total = total + slot[k]
-    return total, copies
+    return total, (everyone, send)
 
 
 def gradient_steps(products):
@@ -228,11 +253,11 @@
     sizes,
     coords_in, polar_in, external_in, live_in, ghost_x_in, ghost_y_in, ghost_z_in,
     pairs_in, alive_in,
-    dipoles, residual,
+    answers,
     coords, polar, external, live, ghost_x, ghost_y, ghost_z, pairs, alive, loads,
-    halo1, halo2, halo3, tabs_y, tabs_z, own_y, own_z, sends, recvs, tab_sends, tab_recvs,
-    order, side, target, window, listed_bits, moved, marks, px, py, pz, inner_s, sums, basis, flat,
-    slot_x, slot_y, slot_z, send_x, send_y, send_z, recv_x, recv_y, recv_z,
+    halo1, halo2, halo3, tabs_y, tabs_z, own_y, own_z, sends, recvs,
+    order, side, target, window, moved, marks, px, py, pz, inner_s, sums, basis, flat,
+    slot_x, slot_y,
 ):
     me = place_of(sizes)
     outside = (
@@ -246,7 +271,7 @@
     ]
     for copy in arriving:
         copy.start()
-    friends = dict.fromkeys(list(OFFSETS) + partners_of(me, sizes))
+    friends = dict.fromkeys(list(OFFSETS) + sum(sum_stages(sizes), []))
     barrier = greet([neighbour(me, sizes, step) for step in friends])
     for copy in arriving:
         copy.wait()
@@ -261,6 +286,16 @@
     lane = iota((1, BLOCK), 1)
     lane_f = lane.astype(jnp.float32)
 
+    lanes_of = site_lanes(
+        site_ranks(
+            [
+                jnp.concatenate(
+                    [coords[k : k + 1, b * BLOCK : (b + 1) * BLOCK] for b in range(NBLK)], axis=0
+                )
+                for k in range(3)
+            ]
+        )
+    )
     for b in range(NBLK):
         cut = slice(b * BLOCK, (b + 1) * BLOCK)
         alpha = polar[0:1, cut]
@@ -273,18 +308,10 @@
         more = jnp.concatenate(
             [living / alpha, living, jnp.zeros((6, BLOCK), jnp.float32)], axis=0
         )
-        column = jnp.transpose(tile)
-        z_row = place[2:3, :]
-        z_col = column[:, 2:3]
-        before = jnp.logical_or(
-            z_row < z_col,
-            jnp.logical_and(z_row == z_col, iota((BLOCK, BLOCK), 1) < iota((BLOCK, BLOCK), 0)),
-        )
-        rank = jnp.sum(before.astype(jnp.float32), axis=1, keepdims=True)
-        one_hot = (rank == iota((BLOCK, BLOCK), 1).astype(jnp.float32)).astype(jnp.float32)
+        one_hot = jnp.where(iota((BLOCK, BLOCK), 0) == lanes_of[b : b + 1, :], 1.0, 0.0)
         one_hot = one_hot.astype(jnp.bfloat16)
         order[b] = one_hot
-        ranked = permuted(dot_rows, jnp.concatenate([tile, more], axis=0), one_hot)
+        ranked = permuted(dot_lanes, jnp.concatenate([tile, more], axis=0), one_hot)
         halo1[1, 1 + b // NBY, 1 + b % NBY] = ranked[:8]
         side[b] = ranked[8:]
         basis[0, b] = jnp.concatenate(
@@ -295,8 +322,7 @@
             target[b * NGRP + g] = flipped[g * GROUP : (g + 1) * GROUP]
 
     pl.semaphore_wait(barrier, len(friends))
-    first = halo_copies(halo1, sends.at[0], recvs.at[0], me, sizes)
-    for copy in first:
+    for copy in halo_copies(halo1, sends.at[0], recvs.at[0], me, sizes):
         copy.start()
 
     for row in range(2):
@@ -306,25 +332,23 @@
     tables = []
     for row, step_y in enumerate((1, -1)):
         for step_z in (-1, 0, 1):
-            n = len(tables)
             tables.append(
                 pltpu.make_async_remote_copy(
                     src_ref=own_y.at[row],
                     dst_ref=tabs_y.at[row, 1 - step_z],
-                    send_sem=tab_sends.at[n],
-                    recv_sem=tab_recvs.at[n],
+                    send_sem=sends.at[3],
+                    recv_sem=recvs.at[3],
                     device_id=neighbour(me, sizes, (0, step_y, step_z)),
                     device_id_type=MESH,
                 )
             )
     for row, step_z in enumerate((1, -1)):
-        n = len(tables)
         tables.append(
             pltpu.make_async_remote_copy(
                 src_ref=own_z.at[row],
                 dst_ref=tabs_z.at[row],
-                send_sem=tab_sends.at[n],
-                recv_sem=tab_recvs.at[n],
+                send_sem=sends.at[3],
+                recv_sem=recvs.at[3],
                 device_id=neighbour(me, sizes, (0, 0, step_z)),
                 device_id_type=MESH,
             )
@@ -338,10 +362,10 @@
     listed = (iota((BLOCK, count), 0) == pairs[1:2, :]).astype(jnp.float32)
     listed_by = dot_lanes(bits, listed.astype(jnp.bfloat16), None)
 
-    for copy in first:
-        copy.wait_recv()
-    for copy in tables:
-        copy.wait_recv()
+    halo_bytes = window.at[pl.ds(0, 3 * NCOL - NBLK)]
+    table_bytes = window.at[pl.ds(0, (6 * 16 + 2 * 24) // 8)]
+    bytes_of(halo_bytes, recvs.at[0]).wait()
+    bytes_of(table_bytes, recvs.at[3]).wait()
 
     for role in range(3):
         for part in range(NCOL // 8):
@@ -393,90 +417,119 @@
             tile = tile + jnp.where(row8 == 2, edge[2][role // 2], 0.0)
         return jnp.where(row8 == 7, marks[role, col : col + 1, :], tile)
 
-    def windows(below, middle, above, lanes):
-        return (
-            jnp.where(lanes >= 80, below, middle),
-            jnp.where(lanes >= 112, below, middle),
-            jnp.where(lanes < 16, above, middle),
-            jnp.where(lanes < 48, above, middle),
-        )
-
-    for cx in range(CX):
-        for cy in range(CY):
-            tiles = windows(*[shifted(role, cx, cy) for role in range(3)], lane8)
-            for g in range(NGRP):
-                for k in range(7):
-                    window[(cx * CY + cy) * NGRP + g, k] = jnp.broadcast_to(
-                        tiles[g][k : k + 1], (8, BLOCK)
-                    )
-                listed_bits[(cx * CY + cy) * NGRP + g] = jnp.broadcast_to(
-                    tiles[g][7:8], (8, BLOCK)
-                ).astype(jnp.int32)
-
-    tiles_of = (GROUP // 8, 8, BLOCK)
-
-    def keep_sums(block, g, total):
+    def windows(tile_at, rows, put):
+        lanes = iota((rows, BLOCK), 1)
+        z_site = jnp.right_shift(lanes, 5) * 2 + (jnp.right_shift(lanes, 2) & 1)
+        x_site = (jnp.right_shift(lanes, 4) & 1) * 2 + (jnp.right_shift(lanes, 1) & 1)
+        y_site = (jnp.right_shift(lanes, 3) & 1) * 2 + (lanes & 1)
+        from_low_x = (x_site >= 1, x_site >= 3)
+        from_low_y = (y_site >= 1, y_site >= 3)
+        layered = {}
+        for cx in range(CX):
+            for cy in range(CY):
+                below, middle, above = [tile_at(role, cx, cy) for role in range(3)]
+                layered[cx, cy] = (
+                    jnp.where(z_site >= 5, below, middle),
+                    jnp.where(z_site >= 7, below, middle),
+                    jnp.where(z_site < 1, above, middle),
+                    jnp.where(z_site < 3, above, middle),
+                )
+        for g in range(NGRP):
+            for bx in range(NBX):
+                mixed_x = [
+                    [
+                        jnp.where(low, layered[bx, cy][g], layered[bx + 2, cy][g])
+                        for cy in range(CY)
+                    ]
+                    for low in from_low_x
+                ]
+                for by in range(NBY):
+                    own = [layered[bx + 1, cy][g] for cy in range(CY)]
+                    tiles = [own[by + 1], mixed_x[0][by + 1], mixed_x[1][by + 1]]
+                    for source in (own, mixed_x[0], mixed_x[1]):
+                        tiles += [jnp.where(low, source[by], source[by + 2]) for low in from_low_y]
+                    for k, tile in enumerate(tiles):
+                        put(((bx * NBY + by) * NGRP + g) * 9 + k, tile)
+
+    def put_window(at, tile):
+        window[at] = tile
+
+    windows(shifted, 8, put_window)
+
+    cubes = [(hx, hy) for hx in range(2) for hy in range(2)]
+
+    def windows_of(hx, hy):
+        return (0, 1 + hx, 3 + hy, 5 + 2 * hx + hy)
+
+    def spread_row(tile, k):
+        return jnp.broadcast_to(tile[k : k + 1], (8, BLOCK))
+
+    def add_field(total, tensor, moment):
+        ax, ay, az, inner = tensor
+        vx, vy, vz = moment
+        along = ax * vx + ay * vy + az * vz
+        parts = [along * a - inner * v for a, v in ((ax, vx), (ay, vy), (az, vz))]
+        return parts if total is None else [t + p for t, p in zip(total, parts)]
+
+    def keep_sums(block, g, u, total):
         for k in range(3):
-            sums[block, k, pl.ds(pl.multiple_of(g * GROUP, GROUP), GROUP)] = total[k].reshape(
-                GROUP, BLOCK
-            )
+            sums[block, k, pl.ds(pl.multiple_of(g * GROUP + u * 8, 8), 8)] = total[k]
 
     def build(step, carry):
         block, g = step // NGRP, step % NGRP
-        column = (block // NBY) * CY + block % NBY
         mine = target[step]
-        tx, ty, tz, tb = [
-            jnp.broadcast_to(mine[:, k : k + 1], (GROUP, BLOCK)).reshape(tiles_of)
-            for k in range(4)
-        ]
-        total = [jnp.zeros(tiles_of, jnp.float32) for _ in range(3)]
-        bit = jnp.left_shift(1, block)
-        for c in range(9):
-            at = (column + (c // 3) * CY + c % 3) * NGRP + g
-            seen = jnp.bitwise_and(listed_bits[at], bit) != 0
-            sx = jnp.where(seen, window[at, 0], FAR)
-            dx, dy, dz = tx - sx[None], ty - window[at, 1][None], tz - window[at, 2][None]
-            if c == 4:
-                mine_at = iota(tiles_of, 0) * 8 + iota(tiles_of, 1) + g * GROUP
-                dx = jnp.where(mine_at == iota(tiles_of, 2), FAR, dx)
-            q = dx * dx + dy * dy + dz * dz
-            inv = lax.rsqrt(q)
-            inv2 = inv * inv
-            margin = jnp.maximum(CUTOFF_SQUARED - q, 0.0)
-            scaled = q * (q * inv) * (tb * window[at, 3][None])
-            damp = jnp.exp(-scaled)
-            rest = 1.0 - damp
-            near = margin * inv2
-            inner = (near * margin) * (inv * rest)
-            root = (3.0 * inv) * (rest - scaled * damp)
-            scale = near * (root * lax.rsqrt(root))
-            ax, ay, az = scale * dx, scale * dy, scale * dz
-            slot = step * 9 + c
-            px[slot], py[slot], pz[slot], inner_s[slot] = ax, ay, az, inner
-            vx, vy, vz = window[at, 4][None], window[at, 5][None], window[at, 6][None]
-            along = ax * vx + ay * vy + az * vz
-            total[0] = total[0] + (along * ax - inner * vx)
-            total[1] = total[1] + (along * ay - inner * vy)
-            total[2] = total[2] + (along * az - inner * vz)
-        keep_sums(block, g, total)
+        sources = []
+        for w in range(9):
+            tile = window[step * 9 + w]
+            seen = jnp.bitwise_and(jnp.right_shift(tile[7:8].astype(jnp.int32), block), 1) == 1
+            sx = jnp.where(seen, tile[0:1], FAR)
+            sources.append(
+                [jnp.broadcast_to(sx, (8, BLOCK))] + [spread_row(tile, k) for k in range(1, 7)]
+            )
+        for u, (hx, hy) in enumerate(cubes):
+            tx, ty, tz, tb = [
+                jnp.broadcast_to(mine[u * 8 : u * 8 + 8, k : k + 1], (8, BLOCK)) for k in range(4)
+            ]
+            total = None
+            for n, w in enumerate(windows_of(hx, hy)):
+                sx, sy, sz, sb, vx, vy, vz = sources[w]
+                dx, dy, dz = tx - sx, ty - sy, tz - sz
+                if n == 0:
+                    itself = row8 + (g * GROUP + u * 8) == lane8
+                    dx = jnp.where(itself, FAR, dx)
+                q = dx * dx + dy * dy + dz * dz
+                inv = lax.rsqrt(q)
+                inv2 = inv * inv
+                margin = jnp.maximum(CUTOFF_SQUARED - q, 0.0)
+                scaled = q * (q * inv) * (tb * sb)
+                damp = jnp.exp(-scaled)
+                rest = 1.0 - damp
+                near = margin * inv2
+                inner = (near * margin) * (inv * rest)
+                root = (3.0 * inv) * (rest - scaled * damp)
+                scale = near * (root * lax.rsqrt(root))
+                tensor = (scale * dx, scale * dy, scale * dz, inner)
+                slot = step * 16 + u * 4 + n
+                px[slot], py[slot], pz[slot], inner_s[slot] = tensor
+                total = add_field(total, tensor, (vx, vy, vz))
+            keep_sums(block, g, u, total)
         return carry
 
     lax.fori_loop(0, NBLK * NGRP, build, 0)
 
     def apply(step, carry):
         block, g = step // NGRP, step % NGRP
-        column = (block // NBY) * CY + block % NBY
-        total = [jnp.zeros(tiles_of, jnp.float32) for _ in range(3)]
-        for c in range(9):
-            at = (column + (c // 3) * CY + c % 3) * NGRP + g
-            slot = step * 9 + c
-            ax, ay, az, inner = px[slot], py[slot], pz[slot], inner_s[slot]
-            vx, vy, vz = moved[at, 0][None], moved[at, 1][None], moved[at, 2][None]
-            along = ax * vx + ay * vy + az * vz
-            total[0] = total[0] + (along * ax - inner * vx)
-            total[1] = total[1] + (along * ay - inner * vy)
-            total[2] = total[2] + (along * az - inner * vz)
-        keep_sums(block, g, total)
+        sources = []
+        for w in range(9):
+            tile = moved[step * 9 + w]
+            sources.append([spread_row(tile, k) for k in range(3)])
+        for u, (hx, hy) in enumerate(cubes):
+            total = None
+            for n, w in enumerate(windows_of(hx, hy)):
+                slot = step * 16 + u * 4 + n
+                tensor = (px[slot], py[slot], pz[slot], inner_s[slot])
+                total = add_field(total, tensor, sources[w])
+            keep_sums(block, g, u, total)
         return carry
 
     ones = jnp.ones((8, BLOCK), jnp.float32)
@@ -504,25 +557,19 @@
             if halo is not None:
                 halo[1, 1 + b // NBY, 1 + b % NBY] = image[:4]
 
-    lane4 = iota((4, BLOCK), 1)
-    started = first + tables
+    def put_moved(at, tile):
+        moved[at] = tile
+
+    started = [(halo_bytes, sends.at[0]), (table_bytes, sends.at[3])]
+    moved_bytes = moved.at[pl.ds(0, 3 * NCOL - NBLK)]
     for level, halo in ((0, halo2), (1, halo3)):
         next_basis(level, halo)
-        copies = halo_copies(halo, sends.at[level + 1], recvs.at[level + 1], me, sizes)
-        for copy in copies:
+        for copy in halo_copies(halo, sends.at[level + 1], recvs.at[level + 1], me, sizes):
             copy.start()
-        for copy in copies:
-            copy.wait_recv()
-        for cx in range(CX):
-            for cy in range(CY):
-                tiles = windows(*[halo[role, cx, cy] for role in range(3)], lane4)
-                for g in range(NGRP):
-                    for k in range(3):
-                        moved[(cx * CY + cy) * NGRP + g, k] = jnp.broadcast_to(
-                            tiles[g][k : k + 1], (8, BLOCK)
-                        )
+        bytes_of(moved_bytes, recvs.at[level + 1]).wait()
+        windows(lambda role, cx, cy, halo=halo: halo[role, cx, cy], 4, put_moved)
         lax.fori_loop(0, NBLK * NGRP, apply, 0)
-        started = started + copies
+        started.append((moved_bytes, sends.at[level + 1]))
     next_basis(2, None)
 
     rows = []
@@ -531,16 +578,16 @@
         rows.append(jnp.sum(part, axis=0, keepdims=True))
     rows.append(jnp.zeros((BLOCK - len(GRAM), BLOCK), jnp.float32))
     total = dot_lanes(ones, jnp.concatenate(rows, axis=0))[0:1]
-    slots, sent, got = (slot_x, slot_y, slot_z), (send_x, send_y, send_z), (recv_x, recv_y, recv_z)
-    for axis, n in enumerate(sizes):
-        total, copies = reduce_along(
-            axis, n, total, slots[axis], sent[axis], got[axis], me, sizes
-        )
-        started = started + copies
-        if axis == 0:
-            for b in range(NBLK):
-                stacked = jnp.concatenate([basis[k, b] for k in range(4)], axis=0)
-                flat[:, b * BLOCK : (b + 1) * BLOCK] = permuted(dot_lanes, stacked, order[b])
+    along, across = sum_stages(sizes)
+    total, sent = reduce_over(along, total, slot_x, me[0], sends.at[4], recvs.at[4], me, sizes)
+    started.append(sent)
+    for b in range(NBLK):
+        stacked = jnp.concatenate([basis[k, b] for k in range(4)], axis=0)
+        flat[:, b * BLOCK : (b + 1) * BLOCK] = permuted(dot_rows, stacked, order[b])
+    total, sent = reduce_over(
+        across, total, slot_y, me[1] * sizes[2] + me[2], sends.at[5], recvs.at[5], me, sizes
+    )
+    started.append(sent)
     products = {}
     for k, (a, b) in enumerate(GRAM):
         products[a, b] = products[b, a] = total[:, k : k + 1]
@@ -553,10 +600,11 @@
                 value = value + c * flat[8 * k : 8 * k + 3, :]
         return value
 
-    dipoles[...] = combined(answer)
-    residual[...] = polar[...] * combined(left)
-    for copy in started:
-        copy.wait_send()
+    answers[...] = jnp.concatenate(
+        [combined(answer), combined(left), jnp.zeros((2, answers.shape[1]), jnp.float32)], axis=0
+    )
+    for view, sem in started:
+        bytes_of(view, sem).wait()
 
 
 def per_device(
@@ -570,13 +618,13 @@
         coords, polarizability.reshape(1, nloc), external_field, bead_live.reshape(1, nloc),
         ghost_x, ghost_y, ghost_z, pair_blocks, pair_live.reshape(1, pair_live.shape[0]),
     )
-    tensors = pltpu.VMEM((NBLK * NGRP * 9, GROUP // 8, 8, BLOCK), f32)
-    steps = len(OFFSETS)
-    return pl.pallas_call(
+    tensors = pltpu.VMEM((NBLK * NGRP * 16, 8, BLOCK), f32)
+    stages = (sizes[0], sizes[1] * sizes[2])
+    answers = pl.pallas_call(
         functools.partial(field_kernel, sizes),
-        out_shape=(jax.ShapeDtypeStruct((3, nloc), f32),) * 2,
+        out_shape=jax.ShapeDtypeStruct((8, nloc), f32),
         in_specs=[pl.BlockSpec(memory_space=pltpu.HBM)] * len(operands),
-        out_specs=(vmem, vmem),
+        out_specs=vmem,
         scratch_shapes=[pltpu.VMEM(x.shape, x.dtype) for x in operands]
         + [
             pltpu.SemaphoreType.DMA((len(operands),)),
@@ -587,28 +635,25 @@
             pltpu.VMEM((2, 24, BLOCK), f32),
             pltpu.VMEM((2, 16, BLOCK), f32),
             pltpu.VMEM((2, 24, BLOCK), f32),
-            pltpu.SemaphoreType.DMA((3, steps)),
-            pltpu.SemaphoreType.DMA((3, steps)),
-            pltpu.SemaphoreType.DMA((8,)),
-            pltpu.SemaphoreType.DMA((8,)),
+            pltpu.SemaphoreType.DMA((6,)),
+            pltpu.SemaphoreType.DMA((6,)),
             pltpu.VMEM((NBLK, BLOCK, BLOCK), jnp.bfloat16),
             pltpu.VMEM((NBLK, 8, BLOCK), f32),
             pltpu.VMEM((NBLK * NGRP, GROUP, 8), f32),
-            pltpu.VMEM((NCOL * NGRP, 7, 8, BLOCK), f32),
-            pltpu.VMEM((NCOL * NGRP, 8, BLOCK), jnp.int32),
-            pltpu.VMEM((NCOL * NGRP, 3, 8, BLOCK), f32),
+            pltpu.VMEM((NBLK * NGRP * 9, 8, BLOCK), f32),
+            pltpu.VMEM((NBLK * NGRP * 9, 4, BLOCK), f32),
             pltpu.VMEM((3, NCOL, BLOCK), f32),
             tensors, tensors, tensors, tensors,
             pltpu.VMEM((NBLK, 3, BLOCK, BLOCK), f32),
             pltpu.VMEM((4, NBLK, 8, BLOCK), f32),
             pltpu.VMEM((32, nloc), f32),
         ]
-        + [pltpu.VMEM((n, 1, BLOCK), f32) for n in sizes]
-        + [pltpu.SemaphoreType.DMA((n - 1,)) for n in sizes] * 2,
+        + [pltpu.VMEM((n, 1, BLOCK), f32) for n in stages],
         compiler_params=pltpu.CompilerParams(
             collective_id=0, has_side_effects=True, vmem_limit_bytes=63 * 2**20
         ),
     )(*operands)
+    return answers[0:3], polarizability[None] * answers[3:6]
 
 
 def solution(mesh):

time: 72.2 us -> 58.7 us (0.81)
  Pallas kernels: 69.4 us -> 56.3 us
  local copies, waits for them, and re-layouts: 1.94 us -> 0.01 us
  other arithmetic: 0 us -> 1.45 us
    pallas_call x1, Pallas kernels: 69.4 us -> 56.3 us  [per_device(): pl.pallas_call(functools.partial(field_kernel, sizes), out_shape=jax.Shap...]
    unnamed x4 -> x2, local copies, waits for them, and re-layouts: 1.94 us -> 0.01 us
    mul x0 -> x1, other arithmetic: none -> 1.45 us  [per_device(): return (answers[0:3], polarizability[None] * answers[3:6])]
where the time goes in v4:
time: 58.7 us; the launch traced here: 58.4 us
  Pallas kernels  56.3 us (96%)
  other arithmetic  1.45 us (2%)
  between operations  0.66 us (1%)
    pallas_call x1, Pallas kernels, per_device(): pl.pallas_call(functools.partial(field_kernel, sizes), out_shape=jax.Shap...  56.3 us
    mul x1, other arithmetic, per_device(): return (answers[0:3], polarizability[None] * answers[3:6])  1.45 us

profile of v4, /device:TPU:1, one launch (start us, length us, event | category | flops | bytes accessed | tf_op | source)
XLA Modules:
  0.0 58.4 jit_solution(5306186700540576963)
XLA Ops:
  0.6 0.0 copy-start
  0.6 56.3 %shard_map.104 = f32[8,1024]{1,0:T(8,128)} custom-call(f32[3,1024]{1,0:T(4,128)} %coords_in.1, f32[1,1024]{1,0:T(1,128)} %bitcast.3, f32[3,1024]{1,0:T(4,128)} %external_in.1, s32[1,1024]{1,0:T(1,128)} %bitcast.4, s32[2,256]{1,0:T(2,128)} %ghost_x_in.1, s32[2,768]{1,0:T(2,128)} %ghost_y_in.1, s32[2,3072]{1,0:T(2,128)} %ghost_z_in.1, s32[2,216]{1,0:T(2,128)} %pairs_in.1, ...), custom_call_target="tpu_custom_call" | custom-call | tf_op jit(solution)/shard_map/pallas_call | solution.py:623
  57.0 0.0 copy-done
  57.0 1.5 %slice_multiply_fusion = (f32[3,1024]{1,0:T(4,128)}, f32[3,1024]{1,0:T(4,128)}) fusion(f32[8,1024]{1,0:T(8,128)} %shard_map.104, f32[1024]{0:T(1024)S(1)} %copy-done), kind=kLoop, calls=%fused_computation | loop fusion | flops 3072 | bytes 53248 | tf_op jit(solution)/shard_map/mul | solution.py:656
Async XLA Ops:
  0.6 56.3 %copy-start = (f32[1024]{0:T(1024)S(1)}, f32[1024]{0:T(1024)}, u32[]{:S(2)}) copy-start(f32[1024]{0:T(1024)} %param.10) | copy-start | bytes 12292

commit v5 on v4

--- a/solution.py
+++ b/solution.py
@@ -157,9 +157,15 @@
     return pltpu.make_async_copy(view, view, sem)
 
 
-def halo_copies(buffer, send_sem, recv_sem, me, sizes):
+def hops(step):
+    return sum(abs(s) for s in step)
+
+
+def halo_copies(buffer, send_sem, recv_sem, me, sizes, distance=None):
     copies = []
-    for step in OFFSETS:
+    for step in sorted(OFFSETS, key=hops, reverse=True):
+        if distance is not None and hops(step) != distance:
+            continue
         (xs, xn), (ys, yn) = own_span(step[0], NBX), own_span(step[1], NBY)
         (xd, _), (yd, _) = halo_span(step[0], NBX), halo_span(step[1], NBY)
         copies.append(
@@ -181,8 +187,7 @@
 
     along = [near((s, 0, 0)) for s in range(1, sizes[0])]
     across = [near((0, y, z)) for y in range(sizes[1]) for z in range(sizes[2]) if y + z > 0]
-    far_first = lambda step: -sum(abs(s) for s in step)
-    return sorted(along, key=far_first), sorted(across, key=far_first)
+    return sorted(along, key=hops, reverse=True), sorted(across, key=hops, reverse=True)
 
 
 def reduce_over(steps, total, slot, place, send, recv, me, sizes):
@@ -201,12 +206,14 @@
         )
     for copy in copies:
         copy.start()
-    everyone = slot.at[pl.ds(0, len(steps))]
-    bytes_of(everyone, recv).wait()
+
+
+def reduced(steps, slot, recv):
+    bytes_of(slot.at[pl.ds(0, len(steps))], recv).wait()
     total = slot[0]
     for k in range(1, len(steps) + 1):
         total = total + slot[k]
-    return total, (everyone, send)
+    return total
 
 
 def gradient_steps(products):
@@ -273,18 +280,7 @@
         copy.start()
     friends = dict.fromkeys(list(OFFSETS) + sum(sum_stages(sizes), []))
     barrier = greet([neighbour(me, sizes, step) for step in friends])
-    for copy in arriving:
-        copy.wait()
-
-    up_blocks, up_lanes = inverse_list(ghost_x, 0, 0, 2 * BLOCK, NBLK)
-    down_blocks, down_lanes = inverse_list(ghost_x, 1, 0, 2 * BLOCK, NBLK)
-    upper = iota((NBLK, BLOCK), 0) >= NBLK - NBY
-    x_spot = jnp.where(
-        upper, (up_blocks - 1.0) * BLOCK + up_lanes, (down_blocks - 1.0) * BLOCK + down_lanes
-    )
-    x_spot = jnp.maximum(x_spot, 0.0)
-    lane = iota((1, BLOCK), 1)
-    lane_f = lane.astype(jnp.float32)
+    arriving[0].wait()
 
     lanes_of = site_lanes(
         site_ranks(
@@ -296,6 +292,19 @@
             ]
         )
     )
+    for copy in arriving[1:]:
+        copy.wait()
+
+    up_blocks, up_lanes = inverse_list(ghost_x, 0, 0, 2 * BLOCK, NBLK)
+    down_blocks, down_lanes = inverse_list(ghost_x, 1, 0, 2 * BLOCK, NBLK)
+    upper = iota((NBLK, BLOCK), 0) >= NBLK - NBY
+    x_spot = jnp.where(
+        upper, (up_blocks - 1.0) * BLOCK + up_lanes, (down_blocks - 1.0) * BLOCK + down_lanes
+    )
+    x_spot = jnp.maximum(x_spot, 0.0)
+    lane = iota((1, BLOCK), 1)
+    lane_f = lane.astype(jnp.float32)
+
     for b in range(NBLK):
         cut = slice(b * BLOCK, (b + 1) * BLOCK)
         alpha = polar[0:1, cut]
@@ -325,36 +334,24 @@
     for copy in halo_copies(halo1, sends.at[0], recvs.at[0], me, sizes):
         copy.start()
 
-    for row in range(2):
+    def send_table(source, landing, step):
+        pltpu.make_async_remote_copy(
+            src_ref=source,
+            dst_ref=landing,
+            send_sem=sends.at[1],
+            recv_sem=recvs.at[1],
+            device_id=neighbour(me, sizes, step),
+            device_id_type=MESH,
+        ).start()
+
+    for row, step_y in enumerate((1, -1)):
         blocks, lanes = inverse_list(ghost_y, row, 0, 6 * BLOCK, 12)
         own_y[row, 0:12] = (blocks - 1.0) * BLOCK + lanes
+        for step_z in (-1, 1, 0):
+            send_table(own_y.at[row], tabs_y.at[row, 1 - step_z], (0, step_y, step_z))
+    for row, step_z in enumerate((1, -1)):
         own_z[row] = inverse_blocks(ghost_z, row, 24 * BLOCK)
-    tables = []
-    for row, step_y in enumerate((1, -1)):
-        for step_z in (-1, 0, 1):
-            tables.append(
-                pltpu.make_async_remote_copy(
-                    src_ref=own_y.at[row],
-                    dst_ref=tabs_y.at[row, 1 - step_z],
-                    send_sem=sends.at[3],
-                    recv_sem=recvs.at[3],
-                    device_id=neighbour(me, sizes, (0, step_y, step_z)),
-                    device_id_type=MESH,
-                )
-            )
-    for row, step_z in enumerate((1, -1)):
-        tables.append(
-            pltpu.make_async_remote_copy(
-                src_ref=own_z.at[row],
-                dst_ref=tabs_z.at[row],
-                send_sem=sends.at[3],
-                recv_sem=recvs.at[3],
-                device_id=neighbour(me, sizes, (0, 0, step_z)),
-                device_id_type=MESH,
-            )
-        )
-    for copy in tables:
-        copy.start()
+        send_table(own_z.at[row], tabs_z.at[row], (0, 0, step_z))
 
     count = pairs.shape[1]
     bits = jnp.left_shift(alive[0:1, :], pairs[0:1, :]).astype(jnp.float32)
@@ -365,7 +362,7 @@
     halo_bytes = window.at[pl.ds(0, 3 * NCOL - NBLK)]
     table_bytes = window.at[pl.ds(0, (6 * 16 + 2 * 24) // 8)]
     bytes_of(halo_bytes, recvs.at[0]).wait()
-    bytes_of(table_bytes, recvs.at[3]).wait()
+    bytes_of(table_bytes, recvs.at[1]).wait()
 
     for role in range(3):
         for part in range(NCOL // 8):
@@ -417,44 +414,57 @@
             tile = tile + jnp.where(row8 == 2, edge[2][role // 2], 0.0)
         return jnp.where(row8 == 7, marks[role, col : col + 1, :], tile)
 
-    def windows(tile_at, rows, put):
+    def windows(tile_at, rows, put, kinds):
         lanes = iota((rows, BLOCK), 1)
         z_site = jnp.right_shift(lanes, 5) * 2 + (jnp.right_shift(lanes, 2) & 1)
         x_site = (jnp.right_shift(lanes, 4) & 1) * 2 + (jnp.right_shift(lanes, 1) & 1)
         y_site = (jnp.right_shift(lanes, 3) & 1) * 2 + (lanes & 1)
-        from_low_x = (x_site >= 1, x_site >= 3)
-        from_low_y = (y_site >= 1, y_site >= 3)
-        layered = {}
-        for cx in range(CX):
-            for cy in range(CY):
+        low_x = (x_site >= 1, x_site >= 3)
+        low_y = (y_site >= 1, y_site >= 3)
+        known = {}
+
+        def layered(cx, cy, g):
+            if (cx, cy) not in known:
                 below, middle, above = [tile_at(role, cx, cy) for role in range(3)]
-                layered[cx, cy] = (
+                known[cx, cy] = (
                     jnp.where(z_site >= 5, below, middle),
                     jnp.where(z_site >= 7, below, middle),
                     jnp.where(z_site < 1, above, middle),
                     jnp.where(z_site < 3, above, middle),
                 )
+            return known[cx, cy][g]
+
+        def mixed_x(bx, half, cy, g):
+            if (bx, half, cy, g) not in known:
+                known[bx, half, cy, g] = jnp.where(
+                    low_x[half], layered(bx, cy, g), layered(bx + 2, cy, g)
+                )
+            return known[bx, half, cy, g]
+
+        def tile_of(kind, bx, by, g):
+            if kind == 0:
+                return layered(bx + 1, by + 1, g)
+            if kind < 3:
+                return mixed_x(bx, kind - 1, by + 1, g)
+            if kind < 5:
+                return jnp.where(
+                    low_y[kind - 3], layered(bx + 1, by, g), layered(bx + 1, by + 2, g)
+                )
+            half_x, half_y = (kind - 5) // 2, (kind - 5) % 2
+            return jnp.where(
+                low_y[half_y], mixed_x(bx, half_x, by, g), mixed_x(bx, half_x, by + 2, g)
+            )
+
         for g in range(NGRP):
             for bx in range(NBX):
-                mixed_x = [
-                    [
-                        jnp.where(low, layered[bx, cy][g], layered[bx + 2, cy][g])
-                        for cy in range(CY)
-                    ]
-                    for low in from_low_x
-                ]
                 for by in range(NBY):
-                    own = [layered[bx + 1, cy][g] for cy in range(CY)]
-                    tiles = [own[by + 1], mixed_x[0][by + 1], mixed_x[1][by + 1]]
-                    for source in (own, mixed_x[0], mixed_x[1]):
-                        tiles += [jnp.where(low, source[by], source[by + 2]) for low in from_low_y]
-                    for k, tile in enumerate(tiles):
-                        put(((bx * NBY + by) * NGRP + g) * 9 + k, tile)
+                    for kind in kinds:
+                        put(((bx * NBY + by) * NGRP + g) * 9 + kind, tile_of(kind, bx, by, g))
 
     def put_window(at, tile):
         window[at] = tile
 
-    windows(shifted, 8, put_window)
+    windows(shifted, 8, put_window, range(9))
 
     cubes = [(hx, hy) for hx in range(2) for hy in range(2)]
 
@@ -515,17 +525,21 @@
             keep_sums(block, g, u, total)
         return carry
 
-    lax.fori_loop(0, NBLK * NGRP, build, 0)
-
-    def apply(step, carry):
+    lax.fori_loop(0, NBLK * NGRP, build, 0, unroll=4)
+
+    def apply(parts, step, carry):
         block, g = step // NGRP, step % NGRP
-        sources = []
-        for w in range(9):
-            tile = moved[step * 9 + w]
-            sources.append([spread_row(tile, k) for k in range(3)])
+        sources = {}
         for u, (hx, hy) in enumerate(cubes):
             total = None
-            for n, w in enumerate(windows_of(hx, hy)):
+            if 0 not in parts:
+                rows = pl.ds(pl.multiple_of(g * GROUP + u * 8, 8), 8)
+                total = [sums[block, k, rows] for k in range(3)]
+            for n in parts:
+                w = windows_of(hx, hy)[n]
+                if w not in sources:
+                    tile = moved[step * 9 + w]
+                    sources[w] = [spread_row(tile, k) for k in range(3)]
                 slot = step * 16 + u * 4 + n
                 tensor = (px[slot], py[slot], pz[slot], inner_s[slot])
                 total = add_field(total, tensor, sources[w])
@@ -560,16 +574,26 @@
     def put_moved(at, tile):
         moved[at] = tile
 
-    started = [(halo_bytes, sends.at[0]), (table_bytes, sends.at[3])]
-    moved_bytes = moved.at[pl.ds(0, 3 * NCOL - NBLK)]
+    started = [(halo_bytes, sends.at[0]), (table_bytes, sends.at[1])]
+    halves_of = {1: 14, 2: 14, 3: 4}
+    works = ((1, (0,), (0,)), (2, (1, 2, 3, 4), (1, 2)), (3, (5, 6, 7, 8), (3,)))
+
+    def put_moved(at, tile):
+        moved[at] = tile
+
     for level, halo in ((0, halo2), (1, halo3)):
         next_basis(level, halo)
-        for copy in halo_copies(halo, sends.at[level + 1], recvs.at[level + 1], me, sizes):
-            copy.start()
-        bytes_of(moved_bytes, recvs.at[level + 1]).wait()
-        windows(lambda role, cx, cy, halo=halo: halo[role, cx, cy], 4, put_moved)
-        lax.fori_loop(0, NBLK * NGRP, apply, 0)
-        started.append((moved_bytes, sends.at[level + 1]))
+        for distance in (3, 2, 1):
+            sem = 2 + 3 * level + distance - 1
+            for copy in halo_copies(halo, sends.at[sem], recvs.at[sem], me, sizes, distance):
+                copy.start()
+        for distance, kinds, parts in works:
+            sem = 2 + 3 * level + distance - 1
+            view = window.at[pl.ds(0, halves_of[distance])]
+            bytes_of(view, recvs.at[sem]).wait()
+            started.append((view, sends.at[sem]))
+            windows(lambda role, cx, cy, halo=halo: halo[role, cx, cy], 4, put_moved, kinds)
+            lax.fori_loop(0, NBLK * NGRP, functools.partial(apply, parts), 0, unroll=4)
     next_basis(2, None)
 
     rows = []
@@ -579,15 +603,16 @@
     rows.append(jnp.zeros((BLOCK - len(GRAM), BLOCK), jnp.float32))
     total = dot_lanes(ones, jnp.concatenate(rows, axis=0))[0:1]
     along, across = sum_stages(sizes)
-    total, sent = reduce_over(along, total, slot_x, me[0], sends.at[4], recvs.at[4], me, sizes)
-    started.append(sent)
+    reduce_over(along, total, slot_x, me[0], sends.at[8], recvs.at[8], me, sizes)
     for b in range(NBLK):
         stacked = jnp.concatenate([basis[k, b] for k in range(4)], axis=0)
         flat[:, b * BLOCK : (b + 1) * BLOCK] = permuted(dot_rows, stacked, order[b])
-    total, sent = reduce_over(
-        across, total, slot_y, me[1] * sizes[2] + me[2], sends.at[5], recvs.at[5], me, sizes
-    )
-    started.append(sent)
+    total = reduced(along, slot_x, recvs.at[8])
+    place = me[1] * sizes[2] + me[2]
+    reduce_over(across, total, slot_y, place, sends.at[9], recvs.at[9], me, sizes)
+    total = reduced(across, slot_y, recvs.at[9])
+    started.append((slot_x.at[pl.ds(0, len(along))], sends.at[8]))
+    started.append((slot_y.at[pl.ds(0, len(across))], sends.at[9]))
     products = {}
     for k, (a, b) in enumerate(GRAM):
         products[a, b] = products[b, a] = total[:, k : k + 1]
@@ -622,7 +647,7 @@
     stages = (sizes[0], sizes[1] * sizes[2])
     answers = pl.pallas_call(
         functools.partial(field_kernel, sizes),
-        out_shape=jax.ShapeDtypeStruct((8, nloc), f32),
+        out_shape=pltpu.VMEM((8, nloc), f32),
         in_specs=[pl.BlockSpec(memory_space=pltpu.HBM)] * len(operands),
         out_specs=vmem,
         scratch_shapes=[pltpu.VMEM(x.shape, x.dtype) for x in operands]
@@ -635,8 +660,8 @@
             pltpu.VMEM((2, 24, BLOCK), f32),
             pltpu.VMEM((2, 16, BLOCK), f32),
             pltpu.VMEM((2, 24, BLOCK), f32),
-            pltpu.SemaphoreType.DMA((6,)),
-            pltpu.SemaphoreType.DMA((6,)),
+            pltpu.SemaphoreType.DMA((10,)),
+            pltpu.SemaphoreType.DMA((10,)),
             pltpu.VMEM((NBLK, BLOCK, BLOCK), jnp.bfloat16),
             pltpu.VMEM((NBLK, 8, BLOCK), f32),
             pltpu.VMEM((NBLK * NGRP, GROUP, 8), f32),

time: 58.7 us -> 54.7 us (0.932)
  Pallas kernels: 56.3 us -> 53.2 us
  other arithmetic: 1.45 us -> 0.62 us
    pallas_call x1, Pallas kernels: 56.3 us -> 53.2 us  [per_device(): pl.pallas_call(functools.partial(field_kernel, sizes), out_shape=pltpu.VM...]
    mul x1, other arithmetic: 1.45 us -> 0.62 us  [per_device(): return (answers[0:3], polarizability[None] * answers[3:6])]
where the time goes in v5:
time: 54.7 us; the launch traced here: 54.5 us
  Pallas kernels  53.2 us (97%)
  between operations  0.66 us (1%)
  other arithmetic  0.62 us (1%)
    pallas_call x1, Pallas kernels, per_device(): pl.pallas_call(functools.partial(field_kernel, sizes), out_shape=pltpu.VM...  53.2 us

profile of v5, /device:TPU:1, one launch (start us, length us, event | category | flops | bytes accessed | tf_op | source)
XLA Modules:
  0.0 54.5 jit_solution(15201166344485049709)
XLA Ops:
  0.6 0.0 copy-start
  0.6 53.2 %shard_map.104 = f32[8,1024]{1,0:T(8,128)S(1)} custom-call(f32[3,1024]{1,0:T(4,128)} %coords_in.1, f32[1,1024]{1,0:T(1,128)} %bitcast.3, f32[3,1024]{1,0:T(4,128)} %external_in.1, s32[1,1024]{1,0:T(1,128)} %bitcast.4, s32[2,256]{1,0:T(2,128)} %ghost_x_in.1, s32[2,768]{1,0:T(2,128)} %ghost_y_in.1, s32[2,3072]{1,0:T(2,128)} %ghost_z_in.1, s32[2,216]{1,0:T(2,128)} %pairs_in.1, ...), custom_call_target="tpu_custom_call" | custom-call | tf_op jit(solution)/shard_map/pallas_call | solution.py:648
  53.9 0.0 copy-done
  53.9 0.6 %slice_multiply_fusion = (f32[3,1024]{1,0:T(4,128)}, f32[3,1024]{1,0:T(4,128)}) fusion(f32[8,1024]{1,0:T(8,128)S(1)} %shard_map.104, f32[1024]{0:T(1024)S(1)} %copy-done), kind=kLoop, calls=%fused_computation | loop fusion | flops 3072 | bytes 53248 | tf_op jit(solution)/shard_map/mul | solution.py:681
Async XLA Ops:
  0.6 53.3 %copy-start = (f32[1024]{0:T(1024)S(1)}, f32[1024]{0:T(1024)}, u32[]{:S(2)}) copy-start(f32[1024]{0:T(1024)} %param.10) | copy-start | bytes 12292

commit v6 on v5

--- a/solution.py
+++ b/solution.py
@@ -264,7 +264,7 @@
     coords, polar, external, live, ghost_x, ghost_y, ghost_z, pairs, alive, loads,
     halo1, halo2, halo3, tabs_y, tabs_z, own_y, own_z, sends, recvs,
     order, side, target, window, moved, marks, px, py, pz, inner_s, sums, basis, flat,
-    slot_x, slot_y,
+    slot_x, slot_y, two_steps, four_steps,
 ):
     me = place_of(sizes)
     outside = (
@@ -278,7 +278,20 @@
     ]
     for copy in arriving:
         copy.start()
-    friends = dict.fromkeys(list(OFFSETS) + sum(sum_stages(sizes), []))
+    chained = sizes[0] == 16 and sizes[1] <= 8 and sizes[2] <= 4
+    friends = dict.fromkeys(list(OFFSETS) + ([] if chained else sum(sum_stages(sizes), [])))
+
+    def relay(sem, reach):
+        if chained:
+            for step in (reach, -reach):
+                pl.semaphore_signal(
+                    sem, inc=1, device_id=neighbour(me, sizes, (step, 0, 0)), device_id_type=MESH
+                )
+
+    def relayed(sem):
+        if chained:
+            pl.semaphore_wait(sem, 2)
+
     barrier = greet([neighbour(me, sizes, step) for step in friends])
     arriving[0].wait()
 
@@ -363,6 +376,7 @@
     table_bytes = window.at[pl.ds(0, (6 * 16 + 2 * 24) // 8)]
     bytes_of(halo_bytes, recvs.at[0]).wait()
     bytes_of(table_bytes, recvs.at[1]).wait()
+    relay(two_steps, 2)
 
     for role in range(3):
         for part in range(NCOL // 8):
@@ -581,28 +595,35 @@
     def put_moved(at, tile):
         moved[at] = tile
 
+    def gram_row(a, b):
+        part = jnp.sum(basis[a] * basis[b], axis=0)
+        return jnp.sum(part, axis=0, keepdims=True)
+
     for level, halo in ((0, halo2), (1, halo3)):
         next_basis(level, halo)
         for distance in (3, 2, 1):
             sem = 2 + 3 * level + distance - 1
             for copy in halo_copies(halo, sends.at[sem], recvs.at[sem], me, sizes, distance):
                 copy.start()
+        if level == 1:
+            early = {(a, b): gram_row(a, b) for a, b in GRAM if b < 3}
         for distance, kinds, parts in works:
             sem = 2 + 3 * level + distance - 1
             view = window.at[pl.ds(0, halves_of[distance])]
             bytes_of(view, recvs.at[sem]).wait()
             started.append((view, sends.at[sem]))
             windows(lambda role, cx, cy, halo=halo: halo[role, cx, cy], 4, put_moved, kinds)
-            lax.fori_loop(0, NBLK * NGRP, functools.partial(apply, parts), 0, unroll=4)
+            lax.fori_loop(0, NBLK * NGRP, functools.partial(apply, parts), 0, unroll=8)
+            if level == 0 and distance == 3:
+                relayed(two_steps)
+                relay(four_steps, 4)
     next_basis(2, None)
 
-    rows = []
-    for a, b in GRAM:
-        part = jnp.sum(basis[a] * basis[b], axis=0)
-        rows.append(jnp.sum(part, axis=0, keepdims=True))
+    rows = [early[a, b] if b < 3 else gram_row(a, b) for a, b in GRAM]
     rows.append(jnp.zeros((BLOCK - len(GRAM), BLOCK), jnp.float32))
     total = dot_lanes(ones, jnp.concatenate(rows, axis=0))[0:1]
     along, across = sum_stages(sizes)
+    relayed(four_steps)
     reduce_over(along, total, slot_x, me[0], sends.at[8], recvs.at[8], me, sizes)
     for b in range(NBLK):
         stacked = jnp.concatenate([basis[k, b] for k in range(4)], axis=0)
@@ -673,7 +694,8 @@
             pltpu.VMEM((4, NBLK, 8, BLOCK), f32),
             pltpu.VMEM((32, nloc), f32),
         ]
-        + [pltpu.VMEM((n, 1, BLOCK), f32) for n in stages],
+        + [pltpu.VMEM((n, 1, BLOCK), f32) for n in stages]
+        + [pltpu.SemaphoreType.REGULAR] * 2,
         compiler_params=pltpu.CompilerParams(
             collective_id=0, has_side_effects=True, vmem_limit_bytes=63 * 2**20
         ),

time: 54.7 us -> 53.2 us (0.973)
  Pallas kernels: 53.2 us -> 51.7 us
    pallas_call x1, Pallas kernels: 53.2 us -> 51.7 us  [per_device(): pl.pallas_call(functools.partial(field_kernel, sizes), out_shape=pltpu.VM...]
where the time goes in v6:
time: 53.2 us; the launch traced here: 53 us
  Pallas kernels  51.7 us (97%)
  between operations  0.66 us (1%)
  other arithmetic  0.62 us (1%)
    pallas_call x1, Pallas kernels, per_device(): pl.pallas_call(functools.partial(field_kernel, sizes), out_shape=pltpu.VM...  51.7 us

profile of v6, /device:TPU:1, one launch (start us, length us, event | category | flops | bytes accessed | tf_op | source)
XLA Modules:
  0.0 53.0 jit_solution(16219702310808173246)
XLA Ops:
  0.6 0.0 copy-start
  0.6 51.7 %shard_map.104 = f32[8,1024]{1,0:T(8,128)S(1)} custom-call(f32[3,1024]{1,0:T(4,128)} %coords_in.1, f32[1,1024]{1,0:T(1,128)} %bitcast.3, f32[3,1024]{1,0:T(4,128)} %external_in.1, s32[1,1024]{1,0:T(1,128)} %bitcast.4, s32[2,256]{1,0:T(2,128)} %ghost_x_in.1, s32[2,768]{1,0:T(2,128)} %ghost_y_in.1, s32[2,3072]{1,0:T(2,128)} %ghost_z_in.1, s32[2,216]{1,0:T(2,128)} %pairs_in.1, ...), custom_call_target="tpu_custom_call" | custom-call | tf_op jit(solution)/shard_map/pallas_call | solution.py:669
  52.4 0.0 copy-done
  52.4 0.6 %slice_multiply_fusion = (f32[3,1024]{1,0:T(4,128)}, f32[3,1024]{1,0:T(4,128)}) fusion(f32[8,1024]{1,0:T(8,128)S(1)} %shard_map.104, f32[1024]{0:T(1024)S(1)} %copy-done), kind=kLoop, calls=%fused_computation | loop fusion | flops 3072 | bytes 53248 | tf_op jit(solution)/shard_map/mul | solution.py:703
Async XLA Ops:
  0.6 51.7 %copy-start = (f32[1024]{0:T(1024)S(1)}, f32[1024]{0:T(1024)}, u32[]{:S(2)}) copy-start(f32[1024]{0:T(1024)} %param.10) | copy-start | bytes 12292

commit v7 on v6

--- a/solution.py
+++ b/solution.py
@@ -539,7 +539,7 @@
             keep_sums(block, g, u, total)
         return carry
 
-    lax.fori_loop(0, NBLK * NGRP, build, 0, unroll=4)
+    lax.fori_loop(0, NBLK * NGRP, build, 0, unroll=8)
 
     def apply(parts, step, carry):
         block, g = step // NGRP, step % NGRP

time: 53.2 us -> 52.9 us (level)
  no operation moved by 1% of the time
where the time goes in v7:
time: 52.9 us; the launch traced here: 52.7 us
  Pallas kernels  51.4 us (97%)
  between operations  0.66 us (1%)
  other arithmetic  0.62 us (1%)
    pallas_call x1, Pallas kernels, per_device(): pl.pallas_call(functools.partial(field_kernel, sizes), out_shape=pltpu.VM...  51.4 us

profile of v7, /device:TPU:1, one launch (start us, length us, event | category | flops | bytes accessed | tf_op | source)
XLA Modules:
  0.0 52.7 jit_solution(16491116529124993839)
XLA Ops:
  0.6 0.0 copy-start
  0.6 51.4 %shard_map.104 = f32[8,1024]{1,0:T(8,128)S(1)} custom-call(f32[3,1024]{1,0:T(4,128)} %coords_in.1, f32[1,1024]{1,0:T(1,128)} %bitcast.3, f32[3,1024]{1,0:T(4,128)} %external_in.1, s32[1,1024]{1,0:T(1,128)} %bitcast.4, s32[2,256]{1,0:T(2,128)} %ghost_x_in.1, s32[2,768]{1,0:T(2,128)} %ghost_y_in.1, s32[2,3072]{1,0:T(2,128)} %ghost_z_in.1, s32[2,216]{1,0:T(2,128)} %pairs_in.1, ...), custom_call_target="tpu_custom_call" | custom-call | tf_op jit(solution)/shard_map/pallas_call | solution.py:669
  52.1 0.0 copy-done
  52.1 0.6 %slice_multiply_fusion = (f32[3,1024]{1,0:T(4,128)}, f32[3,1024]{1,0:T(4,128)}) fusion(f32[8,1024]{1,0:T(8,128)S(1)} %shard_map.104, f32[1024]{0:T(1024)S(1)} %copy-done), kind=kLoop, calls=%fused_computation | loop fusion | flops 3072 | bytes 53248 | tf_op jit(solution)/shard_map/mul | solution.py:703
Async XLA Ops:
  0.6 51.4 %copy-start = (f32[1024]{0:T(1024)S(1)}, f32[1024]{0:T(1024)}, u32[]{:S(2)}) copy-start(f32[1024]{0:T(1024)} %param.10) | copy-start | bytes 12292
